TPU v7x, 128 devices: a whole 4x4x4 slice. The times are simulated.
128 devices in a mesh: noise: 16 (over y_hi, z, core), dp: 8 (over y_lo, x).
Axes of the slice: x: 4, y: 4 (y_hi: 2, y_lo: 2; y = y_hi * 2 + y_lo), z: 4, core: 2. Of those that a mesh axis runs over, the one named last changes fastest.
Arguments:
- noise_latents: float32 [6144, 4096], P(('noise', 'dp')), may hold values from -6.5 to 6.5
- data_latents: float32 [6144, 4096], P(('dp', 'noise')), may hold values from -6.5 to 6.5
Outputs:
- targets: float32 [6144, 4096], P(('noise', 'dp'))
- noise_potential: float32 [6144], P('noise')
- data_potential: float32 [6144], P('dp')
All inputs are finite; a program needn't handle non-finite values.
Results may differ from a plain program's by a relative error of at most 0.0003.
Values sent between devices are 32-bit elements; how exact they have to be, the bound alone decides.
A program may use at most 64 MiB of HBM per device.

v0:
```python
import math

import jax
import jax.numpy as jnp
from jax import lax
from jax.sharding import PartitionSpec as P

ITERS = 3


EPS = 0.01


def row_log_sum(scores):
    top = lax.pmax(jnp.max(scores, axis=1), "dp")
    total = lax.psum(jnp.sum(jnp.exp(scores - top[:, None]), axis=1), "dp")
    return top + jnp.log(total)


def col_log_sum(scores):
    top = lax.pmax(jnp.max(scores, axis=0), "noise")
    total = lax.psum(jnp.sum(jnp.exp(scores - top[None, :]), axis=0), "noise")
    return top + jnp.log(total)


def body(noise_latents, data_latents):
    width = noise_latents.shape[1]
    samples = noise_latents.shape[0] * lax.axis_size("noise") * lax.axis_size("dp")
    log_mass = -math.log(samples)
    columns = lax.all_gather(data_latents, "noise", axis=0, tiled=True)
    col_sq = jnp.sum(columns * columns, axis=1)
    piece = lax.all_gather(noise_latents, "dp", axis=0, tiled=True)
    row_sq = jnp.sum(piece * piece, axis=1)
    cross = lax.dot_general(
        piece,
        columns,
        (((1,), (1,)), ((), ())),
        precision=lax.Precision.HIGHEST,
        preferred_element_type=jnp.float32,
    )
    cost = (row_sq[:, None] + col_sq[None, :] - 2.0 * cross) / width
    data_potential = jnp.zeros((cost.shape[1],), jnp.float32)
    noise_potential = jnp.zeros((cost.shape[0],), jnp.float32)
    for step in range(ITERS):
        noise_potential = -EPS * (row_log_sum((data_potential[None, :] - cost) / EPS) + log_mass)
        data_potential = -EPS * (col_log_sum((noise_potential[:, None] - cost) / EPS) + log_mass)
    logits = (data_potential[None, :] - cost) / EPS
    total = row_log_sum(logits)
    weights = jnp.exp(logits - total[:, None])
    own_rows = noise_latents.shape[0]
    partial_sums = jnp.dot(
        weights, columns, precision=lax.Precision.HIGHEST, preferred_element_type=jnp.float32
    )
    summed = lax.psum(partial_sums, "dp")
    targets = lax.dynamic_slice_in_dim(summed, lax.axis_index("dp") * own_rows, own_rows, 0)
    return (targets, noise_potential, data_potential)


def solution(mesh):
    placed = (P(("noise", "dp"), None), P(("dp", "noise"), None))
    return jax.shard_map(
        body,
        mesh=mesh,
        in_specs=placed,
        out_specs=(P(("noise", "dp"), None), P("noise"), P("dp")),
        check_vma=False,
    )
```

profile of v0, /device:TPU:0, one launch (start us, length us, event | category | flops | bytes accessed | tf_op | source)
XLA Modules:
  0.0 712.0 jit_solution(9449709246859322199)
XLA Ops:
  7.2 0.0 all-gather.3.cloned.1.call-start
  7.2 0.7 all-gather.3.cloned.1.call-update
  7.9 0.0 all-gather.5.cloned.1.call-start
  7.9 0.7 all-gather.5.cloned.1.call-update
  8.6 0.0 all-reduce.2.cloned.1.call-start
  8.7 75.7 %all-gather.3.cloned.1.call-done = f32[384,4096]{1,0:T(8,128)} async-done(((f32[48,4096]{1,0:T(8,128)}), f32[384,4096]{1,0:T(8,128)}) %all-gather.3.cloned.1.call-update) | async-done | bytes 6291472 | tf_op jit(solution)/shard_map/all_gather | solution.py:32
  84.4 3.3 multiply_reduce_fusion.1
  87.6 88.9 %all-gather.5.cloned.1.call-done = f32[768,4096]{1,0:T(8,128)} async-done(((f32[48,4096]{1,0:T(8,128)}), f32[768,4096]{1,0:T(8,128)}) %all-gather.5.cloned.1.call-update) | async-done | bytes 12582928 | tf_op jit(solution)/shard_map/all_gather | solution.py:30
  176.6 0.0 copy-start
  176.6 5.6 multiply_reduce_fusion
  182.2 2.5 copy-done
  184.7 18.1 %fusion.5 = (f32[384]{0:T(512)S(1)}, f32[384,768]{1,0:T(8,128)S(1)}) fusion(f32[384,4096]{1,0:T(8,128)} %all-gather.3.cloned.1.call-done, f32[768,4096]{1,0:T(8,128)S(1)} %copy-done, f32[768]{0:T(1024)S(1)} %multiply_reduce_fusion, f32[384]{0:T(512)S(1)} %multiply_reduce_fusion.1), kind=kOutput, calls=%fused_computation.22 | convolution fusion | flops 14497579008 | bytes 20060160 | tf_op jit(solution)/shard_map/dot_general | solution.py:34
  202.8 18.7 %pmax.49 = f32[384]{0:T(512)S(1)} all-reduce(f32[384]{0:T(512)S(1)} %get-tuple-element.3), channel_id=1, replica_groups=mesh['noise'=16,'dp'=8] {'dp'}, use_global_device_ids=true, to_apply=%region_3.0 | all-reduce | flops 384 | bytes 3072 | tf_op jit(solution)/shard_map/pmax | solution.py:15
  221.5 0.4 exponential_reduce_fusion.6
  221.8 16.0 %psum.56 = f32[384]{0:T(512)S(1)} all-reduce(f32[384]{0:T(512)S(1)} %exponential_reduce_fusion.6), channel_id=1, replica_groups=mesh['noise'=16,'dp'=8] {'dp'}, use_global_device_ids=true, to_apply=%region_5.0 | all-reduce | flops 384 | bytes 3072 | tf_op jit(solution)/shard_map/psum | solution.py:16
  237.8 0.2 fusion.6
  238.0 33.2 %pmax.50 = f32[768]{0:T(1024)S(1)} all-reduce(f32[768]{0:T(1024)S(1)} %fusion.6), channel_id=1, replica_groups=mesh['noise'=16,'dp'=8] {'noise'}, use_global_device_ids=true, to_apply=%region_7.0 | all-reduce | flops 768 | bytes 6144 | tf_op jit(solution)/shard_map/pmax | solution.py:21
  271.2 0.3 exponential_reduce_fusion.5
  271.5 33.2 %psum.57 = f32[768]{0:T(1024)S(1)} all-reduce(f32[768]{0:T(1024)S(1)} %exponential_reduce_fusion.5), channel_id=1, replica_groups=mesh['noise'=16,'dp'=8] {'noise'}, use_global_device_ids=true, to_apply=%region_9.0 | all-reduce | flops 768 | bytes 6144 | tf_op jit(solution)/shard_map/psum | solution.py:22
  304.7 0.2 fusion.7
  304.9 18.0 %pmax.51 = f32[384]{0:T(512)S(1)} all-reduce(f32[384]{0:T(512)S(1)} %fusion.7), channel_id=1, replica_groups=mesh['noise'=16,'dp'=8] {'dp'}, use_global_device_ids=true, to_apply=%region_11.0 | all-reduce | flops 384 | bytes 3072 | tf_op jit(solution)/shard_map/pmax | solution.py:15
  322.8 0.4 exponential_reduce_fusion.4
  323.2 16.0 %psum.58 = f32[384]{0:T(512)S(1)} all-reduce(f32[384]{0:T(512)S(1)} %exponential_reduce_fusion.4), channel_id=1, replica_groups=mesh['noise'=16,'dp'=8] {'dp'}, use_global_device_ids=true, to_apply=%region_13.0 | all-reduce | flops 384 | bytes 3072 | tf_op jit(solution)/shard_map/psum | solution.py:16
  339.2 0.2 fusion.8
  339.4 33.2 %pmax.52 = f32[768]{0:T(1024)S(1)} all-reduce(f32[768]{0:T(1024)S(1)} %fusion.8), channel_id=1, replica_groups=mesh['noise'=16,'dp'=8] {'noise'}, use_global_device_ids=true, to_apply=%region_15.0 | all-reduce | flops 768 | bytes 6144 | tf_op jit(solution)/shard_map/pmax | solution.py:21
  372.5 0.3 exponential_reduce_fusion.3
  372.9 33.2 %psum.59 = f32[768]{0:T(1024)S(1)} all-reduce(f32[768]{0:T(1024)S(1)} %exponential_reduce_fusion.3), channel_id=1, replica_groups=mesh['noise'=16,'dp'=8] {'noise'}, use_global_device_ids=true, to_apply=%region_17.0 | all-reduce | flops 768 | bytes 6144 | tf_op jit(solution)/shard_map/psum | solution.py:22
  406.0 0.2 fusion.9
  406.2 17.9 %pmax.53 = f32[384]{0:T(512)S(1)} all-reduce(f32[384]{0:T(512)S(1)} %fusion.9), channel_id=1, replica_groups=mesh['noise'=16,'dp'=8] {'dp'}, use_global_device_ids=true, to_apply=%region_19.0 | all-reduce | flops 384 | bytes 3072 | tf_op jit(solution)/shard_map/pmax | solution.py:15
  424.2 0.4 exponential_reduce_fusion.2
  424.6 16.0 %psum.60 = f32[384]{0:T(512)S(1)} all-reduce(f32[384]{0:T(512)S(1)} %exponential_reduce_fusion.2), channel_id=1, replica_groups=mesh['noise'=16,'dp'=8] {'dp'}, use_global_device_ids=true, to_apply=%region_21.0 | all-reduce | flops 384 | bytes 3072 | tf_op jit(solution)/shard_map/psum | solution.py:16
  440.5 0.0 copy-start.2
  440.5 0.2 fusion.10
  440.7 33.2 %pmax.54 = f32[768]{0:T(1024)S(1)} all-reduce(f32[768]{0:T(1024)S(1)} %fusion.10), channel_id=1, replica_groups=mesh['noise'=16,'dp'=8] {'noise'}, use_global_device_ids=true, to_apply=%region_23.0 | all-reduce | flops 768 | bytes 6144 | tf_op jit(solution)/shard_map/pmax | solution.py:21
  473.9 0.3 exponential_reduce_fusion.1
  474.2 0.0 copy-done.2
  474.2 33.2 %psum.61 = f32[768]{0:T(1024)S(1)} all-reduce(f32[768]{0:T(1024)S(1)} %exponential_reduce_fusion.1), channel_id=1, replica_groups=mesh['noise'=16,'dp'=8] {'noise'}, use_global_device_ids=true, to_apply=%region_25.0 | all-reduce | flops 768 | bytes 6144 | tf_op jit(solution)/shard_map/psum | solution.py:22
  507.4 0.0 copy-start.1
  507.4 0.2 fusion.11
  507.6 17.9 %pmax.55 = f32[384]{0:T(512)S(1)} all-reduce(f32[384]{0:T(512)S(1)} %fusion.11), channel_id=1, replica_groups=mesh['noise'=16,'dp'=8] {'dp'}, use_global_device_ids=true, to_apply=%region_27.0 | all-reduce | flops 384 | bytes 3072 | tf_op jit(solution)/shard_map/pmax | solution.py:15
  525.6 0.4 exponential_reduce_fusion
  525.9 16.1 %psum.62 = f32[384]{0:T(512)S(1)} all-reduce(f32[384]{0:T(512)S(1)} %exponential_reduce_fusion), channel_id=1, replica_groups=mesh['noise'=16,'dp'=8] {'dp'}, use_global_device_ids=true, to_apply=%region_29.0 | all-reduce | flops 384 | bytes 3072 | tf_op jit(solution)/shard_map/psum | solution.py:16
  542.1 0.0 copy-done.1
  542.1 19.7 %fusion.2 = f32[384,4096]{1,0:T(8,128)} fusion(f32[768,4096]{1,0:T(8,128)} %all-gather.5.cloned.1.call-done, f32[384,768]{1,0:T(8,128)S(1)} %get-tuple-element.4, f32[384]{0:T(512)S(1)} %log_add_fusion, f32[768]{0:T(1024)S(1)} %add_multiply_fusion), kind=kOutput, calls=%fused_computation.5 | convolution fusion | flops 14496399360 | bytes 20058624 | tf_op jit(solution)/shard_map/dot_general | solution.py:51
  561.7 0.0 all-reduce.2.cloned.1.call-update
  561.8 141.7 %all-reduce.2.cloned.1.call-done = f32[384,4096]{1,0:T(8,128)} async-done(((f32[384,4096]{1,0:T(8,128)}), f32[384,4096]{1,0:T(8,128)}) %all-reduce.2.cloned.1.call-update) | async-done | bytes 6291472 | tf_op jit(solution)/shard_map/psum | solution.py:54
  703.4 2.1 constant_dynamic-slice_fusion
  (7 shorter events, 0.1 us)
Async XLA Ops:
  7.2 77.2 %all-gather.3.cloned.1.call-start = ((), (), s32[]{:S(2)}) async-start(), calls=%async_computation | async-start | bytes 7077888 | tf_op jit(solution)/shard_map/all_gather | solution.py:32
  7.9 168.7 %all-gather.5.cloned.1.call-start = ((), (), s32[]{:S(2)}) async-start(), calls=%async_computation.1 | async-start | bytes 13369344 | tf_op jit(solution)/shard_map/all_gather | solution.py:30
  8.6 694.8 %all-reduce.2.cloned.1.call-start = ((), (), s32[]{:S(2)}) async-start(), calls=%async_computation.2 | async-start | bytes 12582912 | tf_op jit(solution)/shard_map/psum | solution.py:54
  176.6 8.2 %copy-start = (f32[768,4096]{1,0:T(8,128)S(1)}, f32[768,4096]{1,0:T(8,128)}, u32[]{:S(2)}) copy-start(f32[768,4096]{1,0:T(8,128)} %all-gather.5.cloned.1.call-done) | copy-start | bytes 37748740
  440.5 33.7 %copy-start.2 = (f32[384]{0:T(512)}, f32[384]{0:T(512)S(1)}, u32[]{:S(2)}) copy-start(f32[384]{0:T(512)S(1)} %add_multiply_fusion.3) | copy-start | bytes 4612
  507.4 34.7 %copy-start.1 = (f32[768]{0:T(1024)}, f32[768]{0:T(1024)S(1)}, u32[]{:S(2)}) copy-start(f32[768]{0:T(1024)S(1)} %add_multiply_fusion) | copy-start | bytes 9220
Sparse Core Ops, SparseCore 0:
  9.6 74.6 all-gather.2
  86.8 89.7 all-gather.4
  561.9 141.5 all-reduce.1
where the time goes:
time: 713 us; the launch traced here: 712 us
  blocking collectives  336 us (47%)
  waiting for transfers between devices  308 us (43%)
  matrix products  37.7 us (5%)
  between operations  13.8 us (2%)
  other arithmetic  12.6 us (2%)
    psum x1, waiting for transfers between devices, body(): summed = lax.psum(partial_sums, 'dp')  142 us
    pmax x3, blocking collectives, col_log_sum(): top = lax.pmax(jnp.max(scores, axis=0), 'noise')  99.5 us
    psum x3, blocking collectives, col_log_sum(): total = lax.psum(jnp.sum(jnp.exp(scores - top[None, :]), axis=0), 'noise')  99.5 us
    all_gather x1, waiting for transfers between devices, body(): columns = lax.all_gather(data_latents, 'noise', axis=0, tiled=True)  88.9 us
    all_gather x1, waiting for transfers between devices, body(): piece = lax.all_gather(noise_latents, 'dp', axis=0, tiled=True)  75.7 us
    pmax x4, blocking collectives, row_log_sum(): top = lax.pmax(jnp.max(scores, axis=1), 'dp')  72.5 us
    psum x4, blocking collectives, row_log_sum(): total = lax.psum(jnp.sum(jnp.exp(scores - top[:, None]), axis=1), 'dp')  64 us
    dot_general x1, matrix products, body(): jnp.dot(weights, columns, precision=lax.Precision.HIGHEST, preferred_elem...  19.7 us
  transfers between devices with their start and end apart: 3, of which 3 were waited for; matrix products, arithmetic and copies ran while one was open for 0% of the time, Pallas kernels for 0%

commit v1 on v0

v1 whole, which is shorter than its diff:
```python
import functools
import math

import jax
import jax.numpy as jnp
from jax import lax
from jax.experimental import pallas as pl
from jax.experimental.pallas import tpu as pltpu
from jax.sharding import PartitionSpec as P

MESH = pl.DeviceIdType.MESH
F32 = jnp.float32
BF16 = jnp.bfloat16
EPS = 0.01

OWN = 48
WIDTH = 4096
HALF = WIDTH // 2
ROWS = 384
COLS = 768
BLK = 96
NB = COLS // BLK
NSAMP = 6144
LOGN = math.log(NSAMP)
SCALE = 1.0 / (WIDTH * EPS)
CH = 4
CW = HALF // CH


def split(v):
    hi = v.astype(BF16)
    return hi, (v - hi.astype(F32)).astype(BF16)


def dot_nt(a, b):
    return lax.dot_general(a, b, (((1,), (1,)), ((), ())), preferred_element_type=F32)


def dot_nn(a, b):
    return lax.dot_general(a, b, (((1,), (0,)), ((), ())), preferred_element_type=F32)


def pack_block(k, val):
    v3 = val.reshape(12, 8, 1)
    lane = lax.broadcasted_iota(jnp.int32, (12, 8, 128), 2)
    lead = lax.broadcasted_iota(jnp.int32, (12, 8, 128), 0) + 12 * k
    return jnp.sum(jnp.where(lane == lead, v3, 0.0), axis=0)


def unpack(packed, first, count):
    lane = lax.broadcasted_iota(jnp.int32, (count, 8, 128), 2)
    lead = lax.broadcasted_iota(jnp.int32, (count, 8, 128), 0) + first
    v3 = jnp.sum(jnp.where(lane == lead, packed[None], 0.0), axis=2, keepdims=True)
    return v3.reshape(8 * count, 1)


def to_row(col):
    r = lax.broadcasted_iota(jnp.int32, (128, 128), 0)
    c = lax.broadcasted_iota(jnp.int32, (128, 128), 1)
    return jnp.sum(jnp.where(r == c, col, 0.0), axis=0, keepdims=True)


def packed_row(packed):
    return jnp.concatenate([to_row(unpack(packed, 16 * q, 16)) for q in range(6)], axis=1)


def rows3(v):
    return [v[:, 128 * q : 128 * q + 128] for q in range(3)]


def flat3(v):
    return jnp.concatenate([v[q : q + 1] for q in range(3)], axis=1)


def kernel(
    x_hbm, y_hbm, t_out, f_out, g_out,
    xb, yb, xh, xl, yh_, yl_, xs, rsq, ps, pr, lg, lo, q_, pn, po, wh, wl, tp, r1, r2, pf,
    rx, cx1, cx, go, vo,
    loc, xr, yr, yr2, prs, lsem, rxs, cx1s, cxs, gs, r1s, r2s, pfs, ssem,
):
    n = lax.axis_index("noise")
    d = lax.axis_index("dp")
    core = lax.rem(n, 2)
    z = lax.rem(n // 2, 4)
    yhi = n // 8
    x = lax.rem(d, 4)
    ylo = d // 4
    h = lax.rem(yhi + ylo, 2)

    def at_z(k):
        return lax.rem(z + k, 4)

    def at_x(k):
        return lax.rem(x + k, 4)

    sib = (n + 1 - 2 * core, d)
    pa = (n, (1 - ylo) * 4 + x)
    pb = (((1 - yhi) * 4 + z) * 2 + core, (1 - ylo) * 4 + x)
    zp = ((yhi * 4 + at_z(1)) * 2 + core, d)
    zm = ((yhi * 4 + at_z(3)) * 2 + core, d)
    xp = (n, ylo * 4 + at_x(1))
    xm = (n, ylo * 4 + at_x(3))

    SRC = {"o": (yhi, ylo), "a": (yhi, 1 - ylo), "b": (1 - yhi, 1 - ylo), "c": (1 - yhi, ylo)}

    def slot(dz, who):
        hi, low = SRC[who]
        return low * 8 + hi * 4 + at_z(dz)

    kmine = pl.ds(pl.multiple_of(h * HALF, HALF), HALF)
    kother = pl.ds(pl.multiple_of((1 - h) * HALF, HALF), HALF)

    cx_own = pltpu.make_async_copy(x_hbm.at[:, kmine], xb.at[d], loc.at[0])
    cy_own = pltpu.make_async_copy(y_hbm.at[:, kmine], yb.at[slot(0, "o"), core], loc.at[1])
    cx_own.start()
    cy_own.start()

    barrier = pltpu.get_barrier_semaphore()

    def greet_dp(k, c):
        pl.semaphore_signal(barrier, inc=1, device_id=(n, lax.rem(d + k, 8)), device_id_type=MESH)
        return c

    def greet_noise(k, c):
        pl.semaphore_signal(barrier, inc=1, device_id=(lax.rem(n + k, 16), d), device_id_type=MESH)
        return c

    lax.fori_loop(1, 8, greet_dp, 0)
    lax.fori_loop(1, 16, greet_noise, 0)
    pl.semaphore_signal(barrier, inc=1, device_id=pb, device_id_type=MESH)
    pl.semaphore_wait(barrier, 23)

    sent = []

    def send(src, dst, rsem, dev):
        c = pltpu.make_async_remote_copy(
            src_ref=src, dst_ref=dst, send_sem=ssem.at[len(sent)], recv_sem=rsem, device_id=dev, device_id_type=MESH
        )
        c.start()
        sent.append(c)
        return c

    def arrived(dst, rsem):
        pltpu.make_async_remote_copy(
            src_ref=dst, dst_ref=dst, send_sem=ssem.at[0], recv_sem=rsem, device_id=sib, device_id_type=MESH
        ).wait_recv()

    def send_y(s, dev):
        return send(yb.at[s, core], yb.at[s, core], yr.at[s], dev)

    def cross_y(s):
        send(yb.at[s, core], yb.at[s, core], yr2.at[s], sib)

    def got_y(s):
        arrived(yb.at[s, core], yr.at[s])
        cross_y(s)

    def send_x(i, dev):
        return send(xb.at[i], xb.at[i], xr.at[i], dev)

    def got_x(i):
        arrived(xb.at[i], xr.at[i])

    xa = (1 - ylo) * 4
    xo = ylo * 4

    to_a = send(x_hbm.at[:, kother], xb.at[d], xr.at[d], pa)
    cx_own.wait()
    send_x(d, xp)
    send_x(d, xm)
    cy_own.wait()
    s = slot(0, "o")
    send_y(s, zp)
    send_y(s, zm)
    send_y(s, pb)
    cross_y(s)

    got_x(xa + x)
    send_x(xa + x, xp)
    send_x(xa + x, xm)
    to_a.wait_send()
    sent.remove(to_a)
    sent.append(None)
    send(y_hbm.at[:, kother], yb.at[slot(0, "o"), core], yr.at[slot(0, "o")], pa)
    got_y(slot(3, "o"))
    send_y(slot(3, "o"), zp)
    got_y(slot(0, "b"))
    send_y(slot(0, "b"), zm)
    got_y(slot(1, "o"))
    got_x(xo + at_x(1))
    got_x(xo + at_x(3))

    got_y(slot(0, "a"))
    send_y(slot(0, "a"), zp)
    send_y(slot(0, "a"), zm)
    send_y(slot(0, "a"), pb)
    got_x(xa + at_x(1))
    send_x(xo + at_x(3), xp)
    send_x(xa + at_x(1), xm)
    got_x(xa + at_x(3))
    got_y(slot(2, "o"))
    got_y(slot(1, "b"))

    def split_x(i, c):
        v = xb[i]
        hi, low = split(v)
        at = pl.ds(pl.multiple_of(i * OWN, OWN), OWN)
        xh[at, :] = hi
        xl[at, :] = low
        xs[at, :] = jnp.broadcast_to(jnp.sum(v * v, axis=1, keepdims=True), (OWN, 128))
        return c

    got_y(slot(0, "c"))
    got_y(slot(3, "a"))
    got_y(slot(1, "a"))
    send_y(slot(1, "a"), zm)
    send_y(slot(0, "b"), zp)
    send_y(slot(2, "o"), pb)
    got_x(xo + at_x(2))
    got_x(xa + at_x(2))
    lax.fori_loop(0, 8, split_x, 0)
    r = lax.broadcasted_iota(jnp.int32, (128, 128), 0)
    c = lax.broadcasted_iota(jnp.int32, (128, 128), 1)
    for i in range(3):
        piece = jnp.sum(jnp.where(r == c, xs[128 * i : 128 * i + 128, :], 0.0), axis=0, keepdims=True)
        rsq[:, 128 * i : 128 * i + 128] = jnp.broadcast_to(piece, (8, 128))

    def block(s):
        arrived(yb.at[s, 1 - core], yr2.at[s])
        v = yb[s].reshape(BLK, HALF)
        hi, low = split(v)
        at = pl.ds(pl.multiple_of(s * BLK, BLK), BLK)
        yh_[at, :] = hi
        yl_[at, :] = low
        csq = jnp.sum(v * v, axis=1, keepdims=True)
        both = dot_nt(jnp.concatenate([hi, low], axis=0), xh[...])
        cross = both[:BLK] + both[BLK:] + dot_nt(hi, xl[...])
        return (2.0 * cross - csq - rsq[0:1, :]) * SCALE

    def pair_block(dz, is_b, idx):
        hi = is_b * (1 - yhi) + (1 - is_b) * yhi
        k = hi * 4 + at_z(dz)
        ps[k] = block((1 - ylo) * 8 + k)
        pltpu.make_async_remote_copy(
            src_ref=ps.at[k], dst_ref=pr.at[k], send_sem=prs.at[0, k], recv_sem=prs.at[1, k], device_id=pa, device_id_type=MESH
        ).start()

    def own_block(dz, is_c):
        hi = is_c * (1 - yhi) + (1 - is_c) * yhi
        k = hi * 4 + at_z(dz)
        lg[pl.ds(pl.multiple_of(k * BLK, BLK), BLK), :] = block(ylo * 8 + k)

    def group1(i, c):
        pair_block(i // 2 + i // 4, (1 - lax.rem(i, 2)) * (1 - i // 4), i)
        return c

    def group2(i, c):
        pair_block(2 + lax.rem(i, 2), (i + 1) // 2, i)
        return c

    def group3(i, c):
        own_block(lax.rem(i, 4), i // 4)
        return c

    def group4(i, c):
        own_block(i + 1, 1)
        return c

    lax.fori_loop(0, 5, group1, 0)
    got_y(slot(2, "a"))
    send_y(slot(2, "a"), pb)
    send_y(slot(0, "c"), zp)
    send_y(slot(0, "c"), zm)
    got_y(slot(3, "b"))
    got_y(slot(2, "b"))
    lax.fori_loop(0, 3, group2, 0)
    lax.fori_loop(0, 5, group3, 0)
    got_y(slot(1, "c"))
    got_y(slot(3, "c"))
    got_y(slot(2, "c"))
    lax.fori_loop(0, 3, group4, 0)

    def pair_wait(k, c):
        d = pltpu.make_async_remote_copy(
            src_ref=ps.at[k], dst_ref=pr.at[k], send_sem=prs.at[0, k], recv_sem=prs.at[1, k], device_id=pa, device_id_type=MESH
        )
        d.wait_recv()
        d.wait_send()
        at = pl.ds(pl.multiple_of(k * BLK, BLK), BLK)
        lg[at, :] = lg[at, :] + pr[k]
        return c

    lax.fori_loop(0, NB, pair_wait, 0)
    send(lg, lo, lsem, pa)

    def ex_rows(rnd, msg):
        rx[rnd, d] = msg

        def go_(k, c):
            p = lax.rem(d + k, 8)
            pltpu.make_async_remote_copy(
                src_ref=rx.at[rnd, d], dst_ref=rx.at[rnd, d], send_sem=rxs.at[0, rnd, p], recv_sem=rxs.at[1, rnd, d],
                device_id=(n, p), device_id_type=MESH,
            ).start()
            return c

        lax.fori_loop(1, 8, go_, 0)

        def done():
            def wt(k, c):
                p = lax.rem(d + k, 8)
                w = pltpu.make_async_remote_copy(
                    src_ref=rx.at[rnd, p], dst_ref=rx.at[rnd, p], send_sem=rxs.at[0, rnd, p], recv_sem=rxs.at[1, rnd, p],
                    device_id=(n, p), device_id_type=MESH,
                )
                w.wait_recv()
                return c

            lax.fori_loop(1, 8, wt, 0)
            return rx[rnd]

        return done

    def ex_cols(buf, sem, msg, rnd):
        buf[rnd, n] = msg

        def go_(k, c):
            p = lax.rem(n + k, 16)
            pltpu.make_async_remote_copy(
                src_ref=buf.at[rnd, n], dst_ref=buf.at[rnd, n], send_sem=sem.at[0, rnd, p], recv_sem=sem.at[1, rnd, n],
                device_id=(p, d), device_id_type=MESH,
            ).start()
            return c

        lax.fori_loop(1, 16, go_, 0)

        def done():
            def wt(k, c):
                p = lax.rem(n + k, 16)
                pltpu.make_async_remote_copy(
                    src_ref=buf.at[rnd, p], dst_ref=buf.at[rnd, p], send_sem=sem.at[0, rnd, p], recv_sem=sem.at[1, rnd, p],
                    device_id=(p, d), device_id_type=MESH,
                ).wait_recv()
                return c

            lax.fori_loop(1, 16, wt, 0)
            return buf[rnd]

        return done

    def row_msg(parts):
        parts = parts + [jnp.zeros((1, 128), F32)] * (8 - len(parts))
        return jnp.concatenate(parts, axis=0)

    def blk(k):
        return slice(BLK * k, BLK * k + BLK)

    def col_max(values):
        m = values[0:8]
        for i in range(1, values.shape[0] // 8):
            m = jnp.maximum(m, values[8 * i : 8 * i + 8])
        return m

    m8 = None
    for k in range(NB):
        piece = jnp.max(lg[blk(k), :].reshape(12, 8, ROWS), axis=0)
        m8 = piece if m8 is None else jnp.maximum(m8, piece)
    m = jnp.max(m8, axis=0, keepdims=True)
    s8 = jnp.zeros((8, ROWS), F32)
    for k in range(NB):
        s8 = s8 + jnp.sum(jnp.exp(lg[blk(k), :] - m).reshape(12, 8, ROWS), axis=0)
    tot = jnp.sum(s8, axis=0, keepdims=True)
    everyone = ex_rows(0, row_msg(rows3(m) + rows3(tot)))()
    mm = everyone[:, 0:3, :]
    top = jnp.max(mm, axis=0)
    tt = jnp.sum(everyone[:, 3:6, :] * jnp.exp(mm - top[None]), axis=0)
    f1 = flat3(LOGN - top - jnp.log(tt))

    pm = jnp.zeros((8, 128), F32)
    pt = jnp.zeros((8, 128), F32)
    for k in range(NB):
        a = lg[blk(k), :] + f1
        cm = jnp.max(a, axis=1, keepdims=True)
        ct = jnp.sum(jnp.exp(a - cm), axis=1, keepdims=True)
        pm = pm + pack_block(k, cm)
        pt = pt + pack_block(k, ct)
    everyone = ex_cols(cx1, cx1s, jnp.concatenate([pm, pt], axis=0), 0)()
    mm = everyone[:, 0:8, :]
    top = jnp.max(mm, axis=0)
    tt = jnp.sum(everyone[:, 8:16, :] * jnp.exp(mm - top[None]), axis=0)
    used = lax.broadcasted_iota(jnp.int32, (8, 128), 1) < 96
    g1 = jnp.where(used, LOGN - top - jnp.log(jnp.where(used, tt, 1.0)), 0.0)
    go[0] = g1
    send(go.at[0], go.at[1], gs.at[0], pa)

    s8 = jnp.zeros((8, ROWS), F32)
    for k in range(NB):
        p = jnp.exp(lg[blk(k), :] + f1 + unpack(g1, 12 * k, 12))
        q_[blk(k), :] = p
        s8 = s8 + jnp.sum(p.reshape(12, 8, ROWS), axis=0)

    def row_step(rnd, s8, between):
        done = ex_rows(rnd, row_msg(rows3(jnp.sum(s8, axis=0, keepdims=True))))
        between()
        return flat3(NSAMP / jnp.sum(done()[:, 0:3, :], axis=0))

    def col_step(rnd, u, between):
        pk = jnp.zeros((8, 128), F32)
        for k in range(NB):
            pk = pk + pack_block(k, jnp.sum(q_[blk(k), :] * u, axis=1, keepdims=True))
        done = ex_cols(cx, cxs, pk, rnd)
        between()
        tt = jnp.sum(done(), axis=0)
        return NSAMP / jnp.where(used, tt, 1.0)

    def row_sums(v):
        s8 = jnp.zeros((8, ROWS), F32)
        for k in range(NB):
            s8 = s8 + jnp.sum((q_[blk(k), :] * unpack(v, 12 * k, 12)).reshape(12, 8, ROWS), axis=0)
        return s8

    def turn(src, dst, some):
        for q in some:
            dst[:, 128 * q : 128 * q + 128] = src[128 * q : 128 * q + 128, :].T

    u = row_step(1, s8, lambda: turn(q_, pn, range(0, 3)))
    v = col_step(0, u, lambda: turn(q_, pn, range(3, 6)))
    u = row_step(2, row_sums(v), lambda: None)

    def other_half():
        arrived(lo, lsem)
        arrived(go.at[1], gs.at[0])
        g2 = go[1]
        for k in range(6):
            at = slice(128 * k, 128 * k + 128)
            po[:, at] = jnp.exp(lo[at, :] + f1 + unpack(g2, 16 * k, 16)).T

    v = col_step(1, u, other_half)
    vo[0] = v
    send(vo.at[0], vo.at[1], gs.at[1], pa)
    total = ex_rows(3, row_msg(rows3(jnp.sum(row_sums(v), axis=0, keepdims=True))))

    hi, low = split(pn[...] * packed_row(v))
    wh[0] = hi
    wl[0] = low

    own_rows = pl.ds(pl.multiple_of(ylo * COLS, COLS), COLS)
    far_rows = pl.ds(pl.multiple_of((1 - ylo) * COLS, COLS), COLS)

    def part(i, rows, cols):
        return (
            dot_nn(wh[i], yh_[rows, cols]) + dot_nn(wh[i], yl_[rows, cols]) + dot_nn(wl[i], yh_[rows, cols])
        )

    def cols_of(c):
        return slice(CW * c, CW * c + CW)

    def compute(c):
        t = part(0, own_rows, cols_of(c))
        if c == 0:
            arrived(vo.at[1], gs.at[1])
            hi, low = split(po[...] * packed_row(vo[1]))
            wh[1] = hi
            wl[1] = low
        t = t + part(1, far_rows, cols_of(c))
        tp[c] = t.reshape(8, OWN, CW)

    def hop1(c):
        send(tp.at[c, xa + at_x(2)], r1.at[c, 0], r1s.at[c, 0], xp)
        send(tp.at[c, xo + at_x(2)], r1.at[c, 1], r1s.at[c, 1], xm)

    def hop2(c):
        send(tp.at[c, xa + at_x(3)], r2.at[c, 0], r2s.at[c, 0], xm)
        arrived(r1.at[c, 0], r1s.at[c, 0])
        tp[c, xa + at_x(1)] = tp[c, xa + at_x(1)] + r1[c, 0]
        send(tp.at[c, xa + at_x(1)], r2.at[c, 1], r2s.at[c, 1], xp)
        arrived(r1.at[c, 1], r1s.at[c, 1])
        tp[c, xo + at_x(3)] = tp[c, xo + at_x(3)] + r1[c, 1]
        send(tp.at[c, xo + at_x(3)], r2.at[c, 2], r2s.at[c, 2], xm)
        send(tp.at[c, xo + at_x(1)], r2.at[c, 3], r2s.at[c, 3], xp)

    def final_pair(c):
        arrived(r2.at[c, 0], r2s.at[c, 0])
        arrived(r2.at[c, 1], r2s.at[c, 1])
        tp[c, xa + x] = tp[c, xa + x] + r2[c, 0] + r2[c, 1]
        send(tp.at[c, xa + x], pf.at[c], pfs.at[c], pa)

    compute(0)
    hop1(0)
    compute(1)
    hop1(1)
    hop2(0)
    compute(2)
    hop1(2)
    hop2(1)
    compute(3)
    hop1(3)
    final_pair(0)
    hop2(2)
    final_pair(1)
    hop2(3)

    fin = flat3(jnp.sum(total()[:, 0:3, :], axis=0))
    lane = lax.broadcasted_iota(jnp.int32, (OWN, ROWS), 1)
    row = lax.broadcasted_iota(jnp.int32, (OWN, ROWS), 0) + d * OWN
    norm = 1.0 / jnp.sum(jnp.where(lane == row, fin, 0.0), axis=1, keepdims=True)
    f_out[...] = EPS * (f1 + jnp.log(u))
    g_out[...] = EPS * packed_row(g1 + jnp.log(v))

    for c in range(2, CH):
        final_pair(c)
    for c in range(CH):
        arrived(r2.at[c, 2], r2s.at[c, 2])
        arrived(r2.at[c, 3], r2s.at[c, 3])
        t = tp[c, xo + x] + r2[c, 2] + r2[c, 3]
        t_out[:, pl.ds(pl.multiple_of(h * HALF + c * CW, CW), CW)] = t * norm
    for c in range(CH):
        arrived(pf.at[c], pfs.at[c])
        t_out[:, pl.ds(pl.multiple_of((1 - h) * HALF + c * CW, CW), CW)] = pf[c] * norm

    for cp in sent:
        if cp is not None:
            cp.wait_send()

    def drain_rows(k, c):
        p = lax.rem(d + k, 8)
        for rnd in range(4):
            pltpu.make_async_remote_copy(
                src_ref=rx.at[rnd, d], dst_ref=rx.at[rnd, d], send_sem=rxs.at[0, rnd, p], recv_sem=rxs.at[1, rnd, d],
                device_id=(n, p), device_id_type=MESH,
            ).wait_send()
        return c

    def drain_cols(k, c):
        p = lax.rem(n + k, 16)
        for buf, sem, rnd in ((cx1, cx1s, 0), (cx, cxs, 0), (cx, cxs, 1)):
            pltpu.make_async_remote_copy(
                src_ref=buf.at[rnd, n], dst_ref=buf.at[rnd, n], send_sem=sem.at[0, rnd, p], recv_sem=sem.at[1, rnd, n],
                device_id=(p, d), device_id_type=MESH,
            ).wait_send()
        return c

    lax.fori_loop(1, 8, drain_rows, 0)
    lax.fori_loop(1, 16, drain_cols, 0)


def body(noise_latents, data_latents):
    dma = pltpu.SemaphoreType.DMA
    vm = pltpu.VMEM
    scratch = [
        vm((8, OWN, HALF), F32),
        vm((16, 2, OWN, HALF), F32),
        vm((ROWS, HALF), BF16),
        vm((ROWS, HALF), BF16),
        vm((2 * COLS, HALF), BF16),
        vm((2 * COLS, HALF), BF16),
        vm((ROWS, 128), F32),
        vm((8, ROWS), F32),
        vm((NB, BLK, ROWS), F32),
        vm((NB, BLK, ROWS), F32),
        vm((COLS, ROWS), F32),
        vm((COLS, ROWS), F32),
        vm((COLS, ROWS), F32),
        vm((ROWS, COLS), F32),
        vm((ROWS, COLS), F32),
        vm((2, ROWS, COLS), BF16),
        vm((2, ROWS, COLS), BF16),
        vm((CH, 8, OWN, CW), F32),
        vm((CH, 2, OWN, CW), F32),
        vm((CH, 4, OWN, CW), F32),
        vm((CH, OWN, CW), F32),
        vm((4, 8, 8, 128), F32),
        vm((1, 16, 16, 128), F32),
        vm((2, 16, 8, 128), F32),
        vm((2, 8, 128), F32),
        vm((2, 8, 128), F32),
        dma((2,)),
        dma((8,)),
        dma((16,)),
        dma((16,)),
        dma((2, NB)),
        dma,
        dma((2, 4, 8)),
        dma((2, 1, 16)),
        dma((2, 2, 16)),
        dma((2,)),
        dma((CH, 2)),
        dma((CH, 4)),
        dma((CH,)),
        dma((96,)),
    ]
    t, f, g = pl.pallas_call(
        kernel,
        out_shape=(
            jax.ShapeDtypeStruct((OWN, WIDTH), F32),
            jax.ShapeDtypeStruct((1, ROWS), F32),
            jax.ShapeDtypeStruct((1, COLS), F32),
        ),
        in_specs=[pl.BlockSpec(memory_space=pl.ANY)] * 2,
        out_specs=(pl.BlockSpec(memory_space=pltpu.VMEM),) * 3,
        scratch_shapes=scratch,
        compiler_params=pltpu.CompilerParams(
            collective_id=0, has_side_effects=True, vmem_limit_bytes=60 * 2**20
        ),
        name="coupling",
    )(noise_latents, data_latents)
    return t, f.reshape(ROWS), g.reshape(COLS)


def solution(mesh):
    placed = (P(("noise", "dp"), None), P(("dp", "noise"), None))
    return jax.shard_map(
        body,
        mesh=mesh,
        in_specs=placed,
        out_specs=(P(("noise", "dp"), None), P("noise"), P("dp")),
        check_vma=False,
    )
```

time: 713 us -> 160 us (0.22)
  blocking collectives: 336 us -> 0 us
  waiting for transfers between devices: 308 us -> 0 us
  Pallas kernels: 0 us -> 156 us
  matrix products: 37.7 us -> 0 us
  between operations: 13.8 us -> 0.66 us
  other arithmetic: 12.6 us -> 1.2 us
    pmax x7 -> x0, blocking collectives: 172 us -> none  [the longest x3 99.5 us: col_log_sum(): top = lax.pmax(jnp.max(scores, axis=0), 'noise')]
    all_gather x2 -> x0, waiting for transfers between devices: 165 us -> none  [the longest x1 88.9 us: body(): columns = lax.all_gather(data_latents, 'noise', axis=0, tiled=True)]
    psum x7 -> x0, blocking collectives: 164 us -> none  [the longest x3 99.5 us: col_log_sum(): total = lax.psum(jnp.sum(jnp.exp(scores - top[None, :]), axis=0), 'noise')]
    pallas_call x0 -> x1, Pallas kernels: none -> 156 us  [body(): pl.pallas_call(kernel, out_shape=(jax.ShapeDtypeStruct((OWN, WIDTH), F32)...]
    psum x1 -> x0, waiting for transfers between devices: 142 us -> none  [body(): summed = lax.psum(partial_sums, 'dp')]
    dot_general x2 -> x0, matrix products: 37.7 us -> none  [the longest x1 19.7 us: body(): jnp.dot(weights, columns, precision=lax.Precision.HIGHEST, preferred_elem...]
    reduce_sum x9 -> x0, other arithmetic: 11.3 us -> none  [the longest x1 5.62 us: body(): col_sq = jnp.sum(columns * columns, axis=1)]
  transfers between devices with their start and end apart: 3 -> 0, of which waited for: 3 -> 0; matrix products, arithmetic and copies ran while one was open for 0% -> 0% of each run, Pallas kernels for 0% -> 0%
where the time goes in v1:
time: 160 us
  Pallas kernels  156 us (98%)
  local copies, waits for them, and re-layouts  2.72 us (2%)
    pallas_call x1, Pallas kernels, body(): pl.pallas_call(kernel, out_shape=(jax.ShapeDtypeStruct((OWN, WIDTH), F32)...  156 us

profile of v1, /device:TPU:0, one launch (start us, length us, event | category | flops | bytes accessed | tf_op | source)
XLA Modules:
  0.0 160.3 jit_solution(5217991845791623051)
XLA Ops:
  0.6 155.7 %coupling.1 = (f32[48,4096]{1,0:T(8,128)}, f32[1,384]{1,0:T(1,128)}, f32[1,768]{1,0:T(1,128)}) custom-call(f32[48,4096]{1,0:T(8,128)} %x_hbm.1, f32[48,4096]{1,0:T(8,128)} %y_hbm.1), custom_call_target="tpu_custom_call" | custom-call | tf_op jit(solution)/shard_map/coupling/pallas_call | solution.py:592
  156.4 0.0 copy-start.1
  156.4 0.0 copy-start
  156.4 0.7 copy-done.1
  157.0 0.6 reduce
  157.6 0.0 copy-done
  157.6 0.6 reduce.1
  158.2 2.1 %copy.6 = f32[48,4096]{1,0:T(8,128)} copy(f32[48,4096]{1,0:T(8,128)} %get-tuple-element.12) | data formatting | bytes 1572864
Async XLA Ops:
  156.4 0.7 copy-start.1
  156.4 1.3 copy-start

commit v2 on v1

--- a/solution.py
+++ b/solution.py
@@ -20,6 +20,8 @@
 COLS = 768
 BLK = 96
 NB = COLS // BLK
+PIECE = OWN // 2
+LO_AT = (0, 320, 576, 768)
 NSAMP = 6144
 LOGN = math.log(NSAMP)
 SCALE = 1.0 / (WIDTH * EPS)
@@ -101,19 +103,27 @@
     xp = (n, ylo * 4 + at_x(1))
     xm = (n, ylo * 4 + at_x(3))
 
-    SRC = {"o": (yhi, ylo), "a": (yhi, 1 - ylo), "b": (1 - yhi, 1 - ylo), "c": (1 - yhi, ylo)}
+    SRC = {"o": (yhi, h), "a": (yhi, 1 - h), "b": (1 - yhi, h), "c": (1 - yhi, 1 - h)}
 
     def slot(dz, who):
-        hi, low = SRC[who]
-        return low * 8 + hi * 4 + at_z(dz)
+        hi, tile = SRC[who]
+        return tile * 8 + hi * 4 + at_z(dz)
+
+    def col_dev(p):
+        return (p, lax.rem(p // 8 + h, 2) * 4 + x)
 
     kmine = pl.ds(pl.multiple_of(h * HALF, HALF), HALF)
     kother = pl.ds(pl.multiple_of((1 - h) * HALF, HALF), HALF)
 
-    cx_own = pltpu.make_async_copy(x_hbm.at[:, kmine], xb.at[d], loc.at[0])
-    cy_own = pltpu.make_async_copy(y_hbm.at[:, kmine], yb.at[slot(0, "o"), core], loc.at[1])
-    cx_own.start()
-    cy_own.start()
+    cx_own = [
+        pltpu.make_async_copy(x_hbm.at[pl.ds(k * PIECE, PIECE), kmine], xb.at[d, k], loc.at[0, k]) for k in range(2)
+    ]
+    cy_own = [
+        pltpu.make_async_copy(y_hbm.at[pl.ds(k * PIECE, PIECE), kmine], yb.at[slot(0, "o"), core, k], loc.at[1, k])
+        for k in range(2)
+    ]
+    for cp in cx_own + cy_own:
+        cp.start()
 
     barrier = pltpu.get_barrier_semaphore()
 
@@ -122,13 +132,12 @@
         return c
 
     def greet_noise(k, c):
-        pl.semaphore_signal(barrier, inc=1, device_id=(lax.rem(n + k, 16), d), device_id_type=MESH)
+        pl.semaphore_signal(barrier, inc=1, device_id=col_dev(lax.rem(n + k, 16)), device_id_type=MESH)
         return c
 
     lax.fori_loop(1, 8, greet_dp, 0)
     lax.fori_loop(1, 16, greet_noise, 0)
-    pl.semaphore_signal(barrier, inc=1, device_id=pb, device_id_type=MESH)
-    pl.semaphore_wait(barrier, 23)
+    pl.semaphore_wait(barrier, 22)
 
     sent = []
 
@@ -145,64 +154,68 @@
             src_ref=dst, dst_ref=dst, send_sem=ssem.at[0], recv_sem=rsem, device_id=sib, device_id_type=MESH
         ).wait_recv()
 
-    def send_y(s, dev):
-        return send(yb.at[s, core], yb.at[s, core], yr.at[s], dev)
-
-    def cross_y(s):
-        send(yb.at[s, core], yb.at[s, core], yr2.at[s], sib)
-
-    def got_y(s):
-        arrived(yb.at[s, core], yr.at[s])
-        cross_y(s)
-
-    def send_x(i, dev):
-        return send(xb.at[i], xb.at[i], xr.at[i], dev)
-
-    def got_x(i):
-        arrived(xb.at[i], xr.at[i])
+    def send_y(s, k, dev):
+        send(yb.at[s, core, k], yb.at[s, core, k], yr.at[s, k], dev)
+
+    def cross_y(s, k):
+        send(yb.at[s, core, k], yb.at[s, core, k], yr2.at[s, k], sib)
+
+    def got_y(s, k):
+        arrived(yb.at[s, core, k], yr.at[s, k])
+        cross_y(s, k)
+
+    def send_x(i, k, dev):
+        send(xb.at[i, k], xb.at[i, k], xr.at[i, k], dev)
+
+    def got_x(i, k):
+        arrived(xb.at[i, k], xr.at[i, k])
 
     xa = (1 - ylo) * 4
     xo = ylo * 4
 
-    to_a = send(x_hbm.at[:, kother], xb.at[d], xr.at[d], pa)
-    cx_own.wait()
-    send_x(d, xp)
-    send_x(d, xm)
-    cy_own.wait()
-    s = slot(0, "o")
-    send_y(s, zp)
-    send_y(s, zm)
-    send_y(s, pb)
-    cross_y(s)
-
-    got_x(xa + x)
-    send_x(xa + x, xp)
-    send_x(xa + x, xm)
-    to_a.wait_send()
-    sent.remove(to_a)
-    sent.append(None)
-    send(y_hbm.at[:, kother], yb.at[slot(0, "o"), core], yr.at[slot(0, "o")], pa)
-    got_y(slot(3, "o"))
-    send_y(slot(3, "o"), zp)
-    got_y(slot(0, "b"))
-    send_y(slot(0, "b"), zm)
-    got_y(slot(1, "o"))
-    got_x(xo + at_x(1))
-    got_x(xo + at_x(3))
-
-    got_y(slot(0, "a"))
-    send_y(slot(0, "a"), zp)
-    send_y(slot(0, "a"), zm)
-    send_y(slot(0, "a"), pb)
-    got_x(xa + at_x(1))
-    send_x(xo + at_x(3), xp)
-    send_x(xa + at_x(1), xm)
-    got_x(xa + at_x(3))
-    got_y(slot(2, "o"))
-    got_y(slot(1, "b"))
+    for k in range(2):
+        send(x_hbm.at[pl.ds(k * PIECE, PIECE), kother], xb.at[d, k], xr.at[d, k], pa)
+    for k in range(2):
+        mine = slot(0, "o")
+        send(y_hbm.at[pl.ds(k * PIECE, PIECE), kother], yb.at[mine, core, k], yr.at[mine, k], pa)
+    for k in range(2):
+        cx_own[k].wait()
+        send_x(d, k, xp)
+        send_x(d, k, xm)
+        cy_own[k].wait()
+        send_y(mine, k, zp)
+        send_y(mine, k, zm)
+        send_y(mine, k, pb)
+        cross_y(mine, k)
+
+    for k in range(2):
+        got_x(xa + x, k)
+        send_x(xa + x, k, xp)
+        send_x(xa + x, k, xm)
+        got_y(slot(3, "o"), k)
+        send_y(slot(3, "o"), k, zp)
+        got_y(slot(0, "b"), k)
+        send_y(slot(0, "b"), k, zm)
+        got_y(slot(1, "o"), k)
+        got_x(xo + at_x(1), k)
+        got_x(xo + at_x(3), k)
+        send_x(xo + at_x(3), k, xp)
+
+    for k in range(2):
+        got_y(slot(0, "a"), k)
+        send_y(slot(0, "a"), k, zp)
+        send_y(slot(0, "a"), k, zm)
+        send_y(slot(0, "a"), k, pb)
+        got_x(xa + at_x(1), k)
+        send_x(xa + at_x(1), k, xm)
+        got_x(xa + at_x(3), k)
+        got_y(slot(2, "o"), k)
+        got_y(slot(1, "b"), k)
+    for k in range(2):
+        send_y(slot(2, "o"), k, pb)
 
     def split_x(i, c):
-        v = xb[i]
+        v = xb[i].reshape(OWN, HALF)
         hi, low = split(v)
         at = pl.ds(pl.multiple_of(i * OWN, OWN), OWN)
         xh[at, :] = hi
@@ -210,14 +223,17 @@
         xs[at, :] = jnp.broadcast_to(jnp.sum(v * v, axis=1, keepdims=True), (OWN, 128))
         return c
 
-    got_y(slot(0, "c"))
-    got_y(slot(3, "a"))
-    got_y(slot(1, "a"))
-    send_y(slot(1, "a"), zm)
-    send_y(slot(0, "b"), zp)
-    send_y(slot(2, "o"), pb)
-    got_x(xo + at_x(2))
-    got_x(xa + at_x(2))
+    for k in range(2):
+        got_y(slot(0, "c"), k)
+        send_y(slot(0, "c"), k, zp)
+        got_y(slot(1, "a"), k)
+        send_y(slot(1, "a"), k, zm)
+        got_y(slot(3, "a"), k)
+        got_x(xo + at_x(2), k)
+        got_x(xa + at_x(2), k)
+    for k in range(2):
+        send_y(slot(0, "b"), k, zp)
+        send_y(slot(0, "c"), k, zm)
     lax.fori_loop(0, 8, split_x, 0)
     r = lax.broadcasted_iota(jnp.int32, (128, 128), 0)
     c = lax.broadcasted_iota(jnp.int32, (128, 128), 1)
@@ -226,7 +242,8 @@
         rsq[:, 128 * i : 128 * i + 128] = jnp.broadcast_to(piece, (8, 128))
 
     def block(s):
-        arrived(yb.at[s, 1 - core], yr2.at[s])
+        for k in range(2):
+            arrived(yb.at[s, 1 - core, k], yr2.at[s, k])
         v = yb[s].reshape(BLK, HALF)
         hi, low = split(v)
         at = pl.ds(pl.multiple_of(s * BLK, BLK), BLK)
@@ -237,25 +254,23 @@
         cross = both[:BLK] + both[BLK:] + dot_nt(hi, xl[...])
         return (2.0 * cross - csq - rsq[0:1, :]) * SCALE
 
-    def pair_block(dz, is_b, idx):
-        hi = is_b * (1 - yhi) + (1 - is_b) * yhi
-        k = hi * 4 + at_z(dz)
-        ps[k] = block((1 - ylo) * 8 + k)
+    def pair_block(dz, is_c):
+        k = (is_c * (1 - yhi) + (1 - is_c) * yhi) * 4 + at_z(dz)
+        ps[k] = block((1 - h) * 8 + k)
         pltpu.make_async_remote_copy(
             src_ref=ps.at[k], dst_ref=pr.at[k], send_sem=prs.at[0, k], recv_sem=prs.at[1, k], device_id=pa, device_id_type=MESH
         ).start()
 
-    def own_block(dz, is_c):
-        hi = is_c * (1 - yhi) + (1 - is_c) * yhi
-        k = hi * 4 + at_z(dz)
-        lg[pl.ds(pl.multiple_of(k * BLK, BLK), BLK), :] = block(ylo * 8 + k)
+    def own_block(dz, is_b):
+        k = (is_b * (1 - yhi) + (1 - is_b) * yhi) * 4 + at_z(dz)
+        lg[pl.ds(pl.multiple_of(k * BLK, BLK), BLK), :] = block(h * 8 + k)
 
     def group1(i, c):
-        pair_block(i // 2 + i // 4, (1 - lax.rem(i, 2)) * (1 - i // 4), i)
+        pair_block(lax.rem(i, 2) + 2 * (i // 3), lax.rem(i // 2 + i // 3, 2))
         return c
 
     def group2(i, c):
-        pair_block(2 + lax.rem(i, 2), (i + 1) // 2, i)
+        pair_block(2 + i, i)
         return c
 
     def group3(i, c):
@@ -263,22 +278,23 @@
         return c
 
     def group4(i, c):
-        own_block(i + 1, 1)
-        return c
-
-    lax.fori_loop(0, 5, group1, 0)
-    got_y(slot(2, "a"))
-    send_y(slot(2, "a"), pb)
-    send_y(slot(0, "c"), zp)
-    send_y(slot(0, "c"), zm)
-    got_y(slot(3, "b"))
-    got_y(slot(2, "b"))
-    lax.fori_loop(0, 3, group2, 0)
-    lax.fori_loop(0, 5, group3, 0)
-    got_y(slot(1, "c"))
-    got_y(slot(3, "c"))
-    got_y(slot(2, "c"))
-    lax.fori_loop(0, 3, group4, 0)
+        pair_block(1 + i, 1)
+        return c
+
+    lax.fori_loop(0, 4, group1, 0)
+    for k in range(2):
+        got_y(slot(2, "a"), k)
+        send_y(slot(2, "a"), k, pb)
+        got_y(slot(3, "c"), k)
+        got_y(slot(2, "b"), k)
+    lax.fori_loop(0, 2, group2, 0)
+    lax.fori_loop(0, 7, group3, 0)
+    for k in range(2):
+        got_y(slot(1, "c"), k)
+        got_y(slot(2, "c"), k)
+        got_y(slot(3, "b"), k)
+    lax.fori_loop(0, 2, group4, 0)
+    own_block(3, 1)
 
     def pair_wait(k, c):
         d = pltpu.make_async_remote_copy(
@@ -291,7 +307,14 @@
         return c
 
     lax.fori_loop(0, NB, pair_wait, 0)
-    send(lg, lo, lsem, pa)
+
+    def send_logits(k):
+        at = pl.ds(LO_AT[k], LO_AT[k + 1] - LO_AT[k])
+        send(lg.at[at], lo.at[at], lsem.at[k], pa)
+
+    def got_logits(k):
+        at = pl.ds(LO_AT[k], LO_AT[k + 1] - LO_AT[k])
+        arrived(lo.at[at], lsem.at[k])
 
     def ex_rows(rnd, msg):
         rx[rnd, d] = msg
@@ -328,7 +351,7 @@
             p = lax.rem(n + k, 16)
             pltpu.make_async_remote_copy(
                 src_ref=buf.at[rnd, n], dst_ref=buf.at[rnd, n], send_sem=sem.at[0, rnd, p], recv_sem=sem.at[1, rnd, n],
-                device_id=(p, d), device_id_type=MESH,
+                device_id=col_dev(p), device_id_type=MESH,
             ).start()
             return c
 
@@ -339,7 +362,7 @@
                 p = lax.rem(n + k, 16)
                 pltpu.make_async_remote_copy(
                     src_ref=buf.at[rnd, p], dst_ref=buf.at[rnd, p], send_sem=sem.at[0, rnd, p], recv_sem=sem.at[1, rnd, p],
-                    device_id=(p, d), device_id_type=MESH,
+                    device_id=col_dev(p), device_id_type=MESH,
                 ).wait_recv()
                 return c
 
@@ -354,12 +377,6 @@
 
     def blk(k):
         return slice(BLK * k, BLK * k + BLK)
-
-    def col_max(values):
-        m = values[0:8]
-        for i in range(1, values.shape[0] // 8):
-            m = jnp.maximum(m, values[8 * i : 8 * i + 8])
-        return m
 
     m8 = None
     for k in range(NB):
@@ -370,7 +387,9 @@
     for k in range(NB):
         s8 = s8 + jnp.sum(jnp.exp(lg[blk(k), :] - m).reshape(12, 8, ROWS), axis=0)
     tot = jnp.sum(s8, axis=0, keepdims=True)
-    everyone = ex_rows(0, row_msg(rows3(m) + rows3(tot)))()
+    done = ex_rows(0, row_msg(rows3(m) + rows3(tot)))
+    send_logits(0)
+    everyone = done()
     mm = everyone[:, 0:3, :]
     top = jnp.max(mm, axis=0)
     tt = jnp.sum(everyone[:, 3:6, :] * jnp.exp(mm - top[None]), axis=0)
@@ -423,19 +442,31 @@
         for q in some:
             dst[:, 128 * q : 128 * q + 128] = src[128 * q : 128 * q + 128, :].T
 
-    u = row_step(1, s8, lambda: turn(q_, pn, range(0, 3)))
+    def far(some):
+        for q in some:
+            at = slice(128 * q, 128 * q + 128)
+            po[:, at] = jnp.exp(lo[at, :] + f1 + unpack(go[1], 16 * q, 16)).T
+
+    def in_row1():
+        send_logits(1)
+        turn(q_, pn, range(0, 3))
+
+    def in_row2():
+        send_logits(2)
+        arrived(go.at[1], gs.at[0])
+        got_logits(0)
+        far(range(0, 2))
+
+    def in_col2():
+        got_logits(1)
+        far(range(2, 4))
+        got_logits(2)
+        far(range(4, 6))
+
+    u = row_step(1, s8, in_row1)
     v = col_step(0, u, lambda: turn(q_, pn, range(3, 6)))
-    u = row_step(2, row_sums(v), lambda: None)
-
-    def other_half():
-        arrived(lo, lsem)
-        arrived(go.at[1], gs.at[0])
-        g2 = go[1]
-        for k in range(6):
-            at = slice(128 * k, 128 * k + 128)
-            po[:, at] = jnp.exp(lo[at, :] + f1 + unpack(g2, 16 * k, 16)).T
-
-    v = col_step(1, u, other_half)
+    u = row_step(2, row_sums(v), in_row2)
+    v = col_step(1, u, in_col2)
     vo[0] = v
     send(vo.at[0], vo.at[1], gs.at[1], pa)
     total = ex_rows(3, row_msg(rows3(jnp.sum(row_sums(v), axis=0, keepdims=True))))
@@ -444,8 +475,8 @@
     wh[0] = hi
     wl[0] = low
 
-    own_rows = pl.ds(pl.multiple_of(ylo * COLS, COLS), COLS)
-    far_rows = pl.ds(pl.multiple_of((1 - ylo) * COLS, COLS), COLS)
+    own_rows = pl.ds(pl.multiple_of(h * COLS, COLS), COLS)
+    far_rows = pl.ds(pl.multiple_of((1 - h) * COLS, COLS), COLS)
 
     def part(i, rows, cols):
         return (
@@ -465,19 +496,23 @@
         t = t + part(1, far_rows, cols_of(c))
         tp[c] = t.reshape(8, OWN, CW)
 
-    def hop1(c):
+    def start_pair(c):
         send(tp.at[c, xa + at_x(2)], r1.at[c, 0], r1s.at[c, 0], xp)
-        send(tp.at[c, xo + at_x(2)], r1.at[c, 1], r1s.at[c, 1], xm)
-
-    def hop2(c):
         send(tp.at[c, xa + at_x(3)], r2.at[c, 0], r2s.at[c, 0], xm)
+
+    def pass_pair(c):
         arrived(r1.at[c, 0], r1s.at[c, 0])
         tp[c, xa + at_x(1)] = tp[c, xa + at_x(1)] + r1[c, 0]
         send(tp.at[c, xa + at_x(1)], r2.at[c, 1], r2s.at[c, 1], xp)
+
+    def start_own(c):
+        send(tp.at[c, xo + at_x(2)], r1.at[c, 1], r1s.at[c, 1], xm)
+        send(tp.at[c, xo + at_x(1)], r2.at[c, 3], r2s.at[c, 3], xp)
+
+    def pass_own(c):
         arrived(r1.at[c, 1], r1s.at[c, 1])
         tp[c, xo + at_x(3)] = tp[c, xo + at_x(3)] + r1[c, 1]
         send(tp.at[c, xo + at_x(3)], r2.at[c, 2], r2s.at[c, 2], xm)
-        send(tp.at[c, xo + at_x(1)], r2.at[c, 3], r2s.at[c, 3], xp)
 
     def final_pair(c):
         arrived(r2.at[c, 0], r2s.at[c, 0])
@@ -485,30 +520,28 @@
         tp[c, xa + x] = tp[c, xa + x] + r2[c, 0] + r2[c, 1]
         send(tp.at[c, xa + x], pf.at[c], pfs.at[c], pa)
 
-    compute(0)
-    hop1(0)
-    compute(1)
-    hop1(1)
-    hop2(0)
-    compute(2)
-    hop1(2)
-    hop2(1)
-    compute(3)
-    hop1(3)
-    final_pair(0)
-    hop2(2)
-    final_pair(1)
-    hop2(3)
+    for c in range(CH):
+        compute(c)
+        start_pair(c)
+        if c:
+            pass_pair(c - 1)
+    pass_pair(CH - 1)
+    for c in range(CH):
+        start_own(c)
 
     fin = flat3(jnp.sum(total()[:, 0:3, :], axis=0))
     lane = lax.broadcasted_iota(jnp.int32, (OWN, ROWS), 1)
     row = lax.broadcasted_iota(jnp.int32, (OWN, ROWS), 0) + d * OWN
     norm = 1.0 / jnp.sum(jnp.where(lane == row, fin, 0.0), axis=1, keepdims=True)
     f_out[...] = EPS * (f1 + jnp.log(u))
-    g_out[...] = EPS * packed_row(g1 + jnp.log(v))
-
-    for c in range(2, CH):
+    near = lax.broadcasted_iota(jnp.int32, (8, 128), 1) // 48 == yhi
+    g_out[...] = EPS * packed_row(jnp.where(near, g1 + jnp.log(v), go[1] + jnp.log(vo[1])))
+
+    for c in range(CH):
         final_pair(c)
+        if c:
+            pass_own(c - 1)
+    pass_own(CH - 1)
     for c in range(CH):
         arrived(r2.at[c, 2], r2s.at[c, 2])
         arrived(r2.at[c, 3], r2s.at[c, 3])
@@ -519,8 +552,7 @@
         t_out[:, pl.ds(pl.multiple_of((1 - h) * HALF + c * CW, CW), CW)] = pf[c] * norm
 
     for cp in sent:
-        if cp is not None:
-            cp.wait_send()
+        cp.wait_send()
 
     def drain_rows(k, c):
         p = lax.rem(d + k, 8)
@@ -536,7 +568,7 @@
         for buf, sem, rnd in ((cx1, cx1s, 0), (cx, cxs, 0), (cx, cxs, 1)):
             pltpu.make_async_remote_copy(
                 src_ref=buf.at[rnd, n], dst_ref=buf.at[rnd, n], send_sem=sem.at[0, rnd, p], recv_sem=sem.at[1, rnd, n],
-                device_id=(p, d), device_id_type=MESH,
+                device_id=col_dev(p), device_id_type=MESH,
             ).wait_send()
         return c
 
@@ -548,8 +580,8 @@
     dma = pltpu.SemaphoreType.DMA
     vm = pltpu.VMEM
     scratch = [
-        vm((8, OWN, HALF), F32),
-        vm((16, 2, OWN, HALF), F32),
+        vm((8, 2, PIECE, HALF), F32),
+        vm((16, 2, 2, PIECE, HALF), F32),
         vm((ROWS, HALF), BF16),
         vm((ROWS, HALF), BF16),
         vm((2 * COLS, HALF), BF16),
@@ -574,12 +606,12 @@
         vm((2, 16, 8, 128), F32),
         vm((2, 8, 128), F32),
         vm((2, 8, 128), F32),
-        dma((2,)),
-        dma((8,)),
-        dma((16,)),
-        dma((16,)),
+        dma((2, 2)),
+        dma((8, 2)),
+        dma((16, 2)),
+        dma((16, 2)),
         dma((2, NB)),
-        dma,
+        dma((3,)),
         dma((2, 4, 8)),
         dma((2, 1, 16)),
         dma((2, 2, 16)),
@@ -587,7 +619,7 @@
         dma((CH, 2)),
         dma((CH, 4)),
         dma((CH,)),
-        dma((96,)),
+        dma((160,)),
     ]
     t, f, g = pl.pallas_call(
         kernel,

time: 160 us -> 142 us (0.89)
  Pallas kernels: 156 us -> 137 us
    pallas_call x1, Pallas kernels: 156 us -> 137 us  [body(): pl.pallas_call(kernel, out_shape=(jax.ShapeDtypeStruct((OWN, WIDTH), F32)...]
where the time goes in v2:
time: 142 us
  Pallas kernels  137 us (96%)
  local copies, waits for them, and re-layouts  2.72 us (2%)
    pallas_call x1, Pallas kernels, body(): pl.pallas_call(kernel, out_shape=(jax.ShapeDtypeStruct((OWN, WIDTH), F32)...  137 us

profile of v2, /device:TPU:0, one launch (start us, length us, event | category | flops | bytes accessed | tf_op | source)
XLA Modules:
  0.0 141.7 jit_solution(11161730575108587257)
XLA Ops:
  0.6 137.1 %coupling.1 = (f32[48,4096]{1,0:T(8,128)}, f32[1,384]{1,0:T(1,128)}, f32[1,768]{1,0:T(1,128)}) custom-call(f32[48,4096]{1,0:T(8,128)} %x_hbm.1, f32[48,4096]{1,0:T(8,128)} %y_hbm.1), custom_call_target="tpu_custom_call" | custom-call | tf_op jit(solution)/shard_map/coupling/pallas_call | solution.py:624
  137.8 0.0 copy-start.1
  137.8 0.0 copy-start
  137.8 0.7 copy-done.1
  138.5 0.6 reduce
  139.1 0.0 copy-done
  139.1 0.6 reduce.1
  139.7 2.1 %copy.6 = f32[48,4096]{1,0:T(8,128)} copy(f32[48,4096]{1,0:T(8,128)} %get-tuple-element.12) | data formatting | bytes 1572864
Async XLA Ops:
  137.8 0.7 copy-start.1
  137.8 1.3 copy-start

commit v3 on v2

--- a/solution.py
+++ b/solution.py
@@ -25,7 +25,7 @@
 NSAMP = 6144
 LOGN = math.log(NSAMP)
 SCALE = 1.0 / (WIDTH * EPS)
-CH = 4
+CH = 8
 CW = HALF // CH
 
 
@@ -76,7 +76,7 @@
 
 def kernel(
     x_hbm, y_hbm, t_out, f_out, g_out,
-    xb, yb, xh, xl, yh_, yl_, xs, rsq, ps, pr, lg, lo, q_, pn, po, wh, wl, tp, r1, r2, pf,
+    xb, yb, xh, xl, yh_, yl_, xs, cs, rsq, ps, pr, lg, lo, q_, pn, po, wh, wl, tp, r1, r2, pf,
     rx, cx1, cx, go, vo,
     loc, xr, yr, yr2, prs, lsem, rxs, cx1s, cxs, gs, r1s, r2s, pfs, ssem,
 ):
@@ -127,17 +127,9 @@
 
     barrier = pltpu.get_barrier_semaphore()
 
-    def greet_dp(k, c):
-        pl.semaphore_signal(barrier, inc=1, device_id=(n, lax.rem(d + k, 8)), device_id_type=MESH)
-        return c
-
-    def greet_noise(k, c):
-        pl.semaphore_signal(barrier, inc=1, device_id=col_dev(lax.rem(n + k, 16)), device_id_type=MESH)
-        return c
-
-    lax.fori_loop(1, 8, greet_dp, 0)
-    lax.fori_loop(1, 16, greet_noise, 0)
-    pl.semaphore_wait(barrier, 22)
+    for dev in (pa, pb, zp, zm, xp, xm, sib):
+        pl.semaphore_signal(barrier, inc=1, device_id=dev, device_id_type=MESH)
+    pl.semaphore_wait(barrier, 7)
 
     sent = []
 
@@ -172,6 +164,29 @@
 
     xa = (1 - ylo) * 4
     xo = ylo * 4
+
+    def split_x(i):
+        v = xb[i].reshape(OWN, HALF)
+        hi, low = split(v)
+        at = pl.ds(pl.multiple_of(i * OWN, OWN), OWN)
+        xh[at, :] = hi
+        xl[at, :] = low
+        xs[at, :] = jnp.broadcast_to(jnp.sum(v * v, axis=1, keepdims=True), (OWN, 128))
+
+    def split_xs(i, c):
+        split_x(at_x(i))
+        split_x(4 + at_x(i))
+        return c
+
+    def split_y(s):
+        for k in range(2):
+            arrived(yb.at[s, 1 - core, k], yr2.at[s, k])
+        v = yb[s].reshape(BLK, HALF)
+        hi, low = split(v)
+        at = pl.ds(pl.multiple_of(s * BLK, BLK), BLK)
+        yh_[at, :] = hi
+        yl_[at, :] = low
+        cs[at, :] = jnp.broadcast_to(jnp.sum(v * v, axis=1, keepdims=True), (BLK, 128))
 
     for k in range(2):
         send(x_hbm.at[pl.ds(k * PIECE, PIECE), kother], xb.at[d, k], xr.at[d, k], pa)
@@ -201,6 +216,8 @@
         got_x(xo + at_x(3), k)
         send_x(xo + at_x(3), k, xp)
 
+    lax.fori_loop(0, 1, split_xs, 0)
+
     for k in range(2):
         got_y(slot(0, "a"), k)
         send_y(slot(0, "a"), k, zp)
@@ -213,15 +230,19 @@
         got_y(slot(1, "b"), k)
     for k in range(2):
         send_y(slot(2, "o"), k, pb)
-
-    def split_x(i, c):
-        v = xb[i].reshape(OWN, HALF)
-        hi, low = split(v)
-        at = pl.ds(pl.multiple_of(i * OWN, OWN), OWN)
-        xh[at, :] = hi
-        xl[at, :] = low
-        xs[at, :] = jnp.broadcast_to(jnp.sum(v * v, axis=1, keepdims=True), (OWN, 128))
-        return c
+    lax.fori_loop(0, 2, lambda i, c: split_xs(1 + 2 * i, c), 0)
+
+    def early(i, c):
+        g = (i + 3) // 4
+        split_y((g * h + (1 - g) * (1 - h)) * 8 + yhi * 4 + at_z(lax.rem(i + 3, 4) * g))
+        return c
+
+    def early2(i, c):
+        split_y(h * 8 + (1 - yhi) * 4 + at_z(i))
+        return c
+
+    lax.fori_loop(0, 5, early, 0)
+    lax.fori_loop(0, 2, early2, 0)
 
     for k in range(2):
         got_y(slot(0, "c"), k)
@@ -234,7 +255,7 @@
     for k in range(2):
         send_y(slot(0, "b"), k, zp)
         send_y(slot(0, "c"), k, zm)
-    lax.fori_loop(0, 8, split_x, 0)
+    lax.fori_loop(2, 3, split_xs, 0)
     r = lax.broadcasted_iota(jnp.int32, (128, 128), 0)
     c = lax.broadcasted_iota(jnp.int32, (128, 128), 1)
     for i in range(3):
@@ -242,31 +263,29 @@
         rsq[:, 128 * i : 128 * i + 128] = jnp.broadcast_to(piece, (8, 128))
 
     def block(s):
-        for k in range(2):
-            arrived(yb.at[s, 1 - core, k], yr2.at[s, k])
-        v = yb[s].reshape(BLK, HALF)
-        hi, low = split(v)
         at = pl.ds(pl.multiple_of(s * BLK, BLK), BLK)
-        yh_[at, :] = hi
-        yl_[at, :] = low
-        csq = jnp.sum(v * v, axis=1, keepdims=True)
-        both = dot_nt(jnp.concatenate([hi, low], axis=0), xh[...])
+        hi = yh_[at, :]
+        both = dot_nt(jnp.concatenate([hi, yl_[at, :]], axis=0), xh[...])
         cross = both[:BLK] + both[BLK:] + dot_nt(hi, xl[...])
-        return (2.0 * cross - csq - rsq[0:1, :]) * SCALE
-
-    def pair_block(dz, is_c):
+        return (2.0 * cross - cs[at, 0:1] - rsq[0:1, :]) * SCALE
+
+    def pair_block(dz, is_c, ready=False):
         k = (is_c * (1 - yhi) + (1 - is_c) * yhi) * 4 + at_z(dz)
+        if not ready:
+            split_y((1 - h) * 8 + k)
         ps[k] = block((1 - h) * 8 + k)
         pltpu.make_async_remote_copy(
             src_ref=ps.at[k], dst_ref=pr.at[k], send_sem=prs.at[0, k], recv_sem=prs.at[1, k], device_id=pa, device_id_type=MESH
         ).start()
 
-    def own_block(dz, is_b):
+    def own_block(dz, is_b, ready=False):
         k = (is_b * (1 - yhi) + (1 - is_b) * yhi) * 4 + at_z(dz)
+        if not ready:
+            split_y(h * 8 + k)
         lg[pl.ds(pl.multiple_of(k * BLK, BLK), BLK), :] = block(h * 8 + k)
 
     def group1(i, c):
-        pair_block(lax.rem(i, 2) + 2 * (i // 3), lax.rem(i // 2 + i // 3, 2))
+        pair_block(lax.rem(1 + 2 * i, 4) * (1 - i // 2), i // 2)
         return c
 
     def group2(i, c):
@@ -274,27 +293,32 @@
         return c
 
     def group3(i, c):
-        own_block(lax.rem(i, 4), i // 4)
+        own_block(lax.rem(i, 4), i // 4, True)
         return c
 
     def group4(i, c):
         pair_block(1 + i, 1)
         return c
 
-    lax.fori_loop(0, 4, group1, 0)
+    def group5(i, c):
+        own_block(2 + i, 1)
+        return c
+
+    pair_block(0, 0, True)
+    lax.fori_loop(0, 3, group1, 0)
     for k in range(2):
         got_y(slot(2, "a"), k)
         send_y(slot(2, "a"), k, pb)
         got_y(slot(3, "c"), k)
         got_y(slot(2, "b"), k)
     lax.fori_loop(0, 2, group2, 0)
-    lax.fori_loop(0, 7, group3, 0)
+    lax.fori_loop(0, 6, group3, 0)
     for k in range(2):
         got_y(slot(1, "c"), k)
         got_y(slot(2, "c"), k)
         got_y(slot(3, "b"), k)
     lax.fori_loop(0, 2, group4, 0)
-    own_block(3, 1)
+    lax.fori_loop(0, 2, group5, 0)
 
     def pair_wait(k, c):
         d = pltpu.make_async_remote_copy(
@@ -576,6 +600,18 @@
     lax.fori_loop(1, 16, drain_cols, 0)
 
 
+def hand_out(t_in, f_in, g_in, t_out, f_out, g_out, sem):
+    parts = [
+        pltpu.make_async_copy(t_in.at[pl.ds(8 * k, 8)], t_out.at[pl.ds(8 * k, 8)], sem.at[k]) for k in range(OWN // 8)
+    ]
+    for cp in parts:
+        cp.start()
+    f_out[...] = f_in[...].reshape(ROWS)
+    g_out[...] = g_in[...].reshape(COLS)
+    for cp in parts:
+        cp.wait()
+
+
 def body(noise_latents, data_latents):
     dma = pltpu.SemaphoreType.DMA
     vm = pltpu.VMEM
@@ -587,6 +623,7 @@
         vm((2 * COLS, HALF), BF16),
         vm((2 * COLS, HALF), BF16),
         vm((ROWS, 128), F32),
+        vm((2 * COLS, 128), F32),
         vm((8, ROWS), F32),
         vm((NB, BLK, ROWS), F32),
         vm((NB, BLK, ROWS), F32),
@@ -619,14 +656,14 @@
         dma((CH, 2)),
         dma((CH, 4)),
         dma((CH,)),
-        dma((160,)),
+        dma((192,)),
     ]
     t, f, g = pl.pallas_call(
         kernel,
         out_shape=(
-            jax.ShapeDtypeStruct((OWN, WIDTH), F32),
-            jax.ShapeDtypeStruct((1, ROWS), F32),
-            jax.ShapeDtypeStruct((1, COLS), F32),
+            vm((OWN, WIDTH), F32),
+            vm((1, ROWS), F32),
+            vm((1, COLS), F32),
         ),
         in_specs=[pl.BlockSpec(memory_space=pl.ANY)] * 2,
         out_specs=(pl.BlockSpec(memory_space=pltpu.VMEM),) * 3,
@@ -636,7 +673,18 @@
         ),
         name="coupling",
     )(noise_latents, data_latents)
-    return t, f.reshape(ROWS), g.reshape(COLS)
+    return pl.pallas_call(
+        hand_out,
+        out_shape=(
+            jax.ShapeDtypeStruct((OWN, WIDTH), F32),
+            jax.ShapeDtypeStruct((ROWS,), F32),
+            jax.ShapeDtypeStruct((COLS,), F32),
+        ),
+        in_specs=[pl.BlockSpec(memory_space=pltpu.VMEM)] * 3,
+        out_specs=(pl.BlockSpec(memory_space=pl.ANY),) + (pl.BlockSpec(memory_space=pltpu.VMEM),) * 2,
+        scratch_shapes=[pltpu.SemaphoreType.DMA((OWN // 8,))],
+        name="hand_out",
+    )(t, f, g)
 
 
 def solution(mesh):

time: 142 us -> 145 us (1.021)
  Pallas kernels: 137 us -> 142 us
    pallas_call x1 -> x2, Pallas kernels: 137 us -> 142 us  [the longest x1 139 us: body(): pl.pallas_call(kernel, out_shape=(vm((OWN, WIDTH), F32), vm((1, ROWS), F3...]
where the time goes in v3:
time: 145 us
  Pallas kernels  142 us (98%)
  local copies, waits for them, and re-layouts  2.03 us (1%)
    pallas_call x1, Pallas kernels, body(): pl.pallas_call(kernel, out_shape=(vm((OWN, WIDTH), F32), vm((1, ROWS), F3...  139 us

profile of v3, /device:TPU:0, one launch (start us, length us, event | category | flops | bytes accessed | tf_op | source)
XLA Modules:
  0.0 144.6 jit_solution(13371738628150932950)
XLA Ops:
  0.6 139.1 %coupling.1 = (f32[48,4096]{1,0:T(8,128)S(1)}, f32[1,384]{1,0:T(1,128)S(1)}, f32[1,768]{1,0:T(1,128)S(1)}) custom-call(f32[48,4096]{1,0:T(8,128)} %x_hbm.1, f32[48,4096]{1,0:T(8,128)} %y_hbm.1), custom_call_target="tpu_custom_call" | custom-call | tf_op jit(solution)/shard_map/coupling/pallas_call | solution.py:661
  139.7 0.0 copy-start
  139.8 0.9 copy-done
  140.6 0.0 copy-start.2
  140.6 0.6 copy-done.2
  141.2 0.0 copy-start.1
  141.2 0.6 copy-done.1
  141.8 2.6 %hand_out.1 = (f32[48,4096]{1,0:T(8,128)}, f32[384]{0:T(512)}, f32[768]{0:T(1024)}) custom-call(f32[48,4096]{1,0:T(8,128)} %copy-done, f32[1,384]{1,0:T(1,128)} %copy-done.2, f32[1,768]{1,0:T(1,128)} %copy-done.1), custom_call_target="tpu_custom_call" | custom-call | tf_op jit(solution)/shard_map/hand_out/pallas_call | solution.py:676
Async XLA Ops:
  139.7 0.9 copy-start
  140.6 0.6 copy-start.2
  141.2 0.6 copy-start.1

commit v4 on v3

--- a/solution.py
+++ b/solution.py
@@ -25,7 +25,7 @@
 NSAMP = 6144
 LOGN = math.log(NSAMP)
 SCALE = 1.0 / (WIDTH * EPS)
-CH = 8
+CH = 4
 CW = HALF // CH
 
 
@@ -76,7 +76,7 @@
 
 def kernel(
     x_hbm, y_hbm, t_out, f_out, g_out,
-    xb, yb, xh, xl, yh_, yl_, xs, cs, rsq, ps, pr, lg, lo, q_, pn, po, wh, wl, tp, r1, r2, pf,
+    xb, yb, xh, xl, yh_, yl_, xs, rsq, ps, pr, lg, lo, q_, pn, po, wh, wl, tp, r1, r2, pf,
     rx, cx1, cx, go, vo,
     loc, xr, yr, yr2, prs, lsem, rxs, cx1s, cxs, gs, r1s, r2s, pfs, ssem,
 ):
@@ -186,7 +186,7 @@
         at = pl.ds(pl.multiple_of(s * BLK, BLK), BLK)
         yh_[at, :] = hi
         yl_[at, :] = low
-        cs[at, :] = jnp.broadcast_to(jnp.sum(v * v, axis=1, keepdims=True), (BLK, 128))
+        return hi, low, jnp.sum(v * v, axis=1, keepdims=True)
 
     for k in range(2):
         send(x_hbm.at[pl.ds(k * PIECE, PIECE), kother], xb.at[d, k], xr.at[d, k], pa)
@@ -232,18 +232,6 @@
         send_y(slot(2, "o"), k, pb)
     lax.fori_loop(0, 2, lambda i, c: split_xs(1 + 2 * i, c), 0)
 
-    def early(i, c):
-        g = (i + 3) // 4
-        split_y((g * h + (1 - g) * (1 - h)) * 8 + yhi * 4 + at_z(lax.rem(i + 3, 4) * g))
-        return c
-
-    def early2(i, c):
-        split_y(h * 8 + (1 - yhi) * 4 + at_z(i))
-        return c
-
-    lax.fori_loop(0, 5, early, 0)
-    lax.fori_loop(0, 2, early2, 0)
-
     for k in range(2):
         got_y(slot(0, "c"), k)
         send_y(slot(0, "c"), k, zp)
@@ -263,29 +251,24 @@
         rsq[:, 128 * i : 128 * i + 128] = jnp.broadcast_to(piece, (8, 128))
 
     def block(s):
-        at = pl.ds(pl.multiple_of(s * BLK, BLK), BLK)
-        hi = yh_[at, :]
-        both = dot_nt(jnp.concatenate([hi, yl_[at, :]], axis=0), xh[...])
+        hi, low, csq = split_y(s)
+        both = dot_nt(jnp.concatenate([hi, low], axis=0), xh[...])
         cross = both[:BLK] + both[BLK:] + dot_nt(hi, xl[...])
-        return (2.0 * cross - cs[at, 0:1] - rsq[0:1, :]) * SCALE
-
-    def pair_block(dz, is_c, ready=False):
+        return (2.0 * cross - csq - rsq[0:1, :]) * SCALE
+
+    def pair_block(dz, is_c):
         k = (is_c * (1 - yhi) + (1 - is_c) * yhi) * 4 + at_z(dz)
-        if not ready:
-            split_y((1 - h) * 8 + k)
         ps[k] = block((1 - h) * 8 + k)
         pltpu.make_async_remote_copy(
             src_ref=ps.at[k], dst_ref=pr.at[k], send_sem=prs.at[0, k], recv_sem=prs.at[1, k], device_id=pa, device_id_type=MESH
         ).start()
 
-    def own_block(dz, is_b, ready=False):
+    def own_block(dz, is_b):
         k = (is_b * (1 - yhi) + (1 - is_b) * yhi) * 4 + at_z(dz)
-        if not ready:
-            split_y(h * 8 + k)
         lg[pl.ds(pl.multiple_of(k * BLK, BLK), BLK), :] = block(h * 8 + k)
 
     def group1(i, c):
-        pair_block(lax.rem(1 + 2 * i, 4) * (1 - i // 2), i // 2)
+        pair_block(lax.rem(i, 2) + 2 * (i // 3), lax.rem(i // 2 + i // 3, 2))
         return c
 
     def group2(i, c):
@@ -293,7 +276,7 @@
         return c
 
     def group3(i, c):
-        own_block(lax.rem(i, 4), i // 4, True)
+        own_block(lax.rem(i, 4), i // 4)
         return c
 
     def group4(i, c):
@@ -304,8 +287,7 @@
         own_block(2 + i, 1)
         return c
 
-    pair_block(0, 0, True)
-    lax.fori_loop(0, 3, group1, 0)
+    lax.fori_loop(0, 4, group1, 0)
     for k in range(2):
         got_y(slot(2, "a"), k)
         send_y(slot(2, "a"), k, pb)
@@ -623,7 +605,6 @@
         vm((2 * COLS, HALF), BF16),
         vm((2 * COLS, HALF), BF16),
         vm((ROWS, 128), F32),
-        vm((2 * COLS, 128), F32),
         vm((8, ROWS), F32),
         vm((NB, BLK, ROWS), F32),
         vm((NB, BLK, ROWS), F32),
@@ -683,6 +664,7 @@
         in_specs=[pl.BlockSpec(memory_space=pltpu.VMEM)] * 3,
         out_specs=(pl.BlockSpec(memory_space=pl.ANY),) + (pl.BlockSpec(memory_space=pltpu.VMEM),) * 2,
         scratch_shapes=[pltpu.SemaphoreType.DMA((OWN // 8,))],
+        compiler_params=pltpu.CompilerParams(vmem_limit_bytes=2 * 2**20),
         name="hand_out",
     )(t, f, g)
 

time: 145 us -> 135 us (0.931)
  Pallas kernels: 142 us -> 133 us
  local copies, waits for them, and re-layouts: 2.03 us -> 0 us
    pallas_call x1, Pallas kernels: 139 us -> 132 us  [body(): pl.pallas_call(kernel, out_shape=(vm((OWN, WIDTH), F32), vm((1, ROWS), F3...]
    unnamed x6 -> x0, local copies, waits for them, and re-layouts: 2.03 us -> none
where the time goes in v4:
time: 135 us; the launch traced here: 134 us
  Pallas kernels  133 us (99%)
    pallas_call x1, Pallas kernels, body(): pl.pallas_call(kernel, out_shape=(vm((OWN, WIDTH), F32), vm((1, ROWS), F3...  132 us

profile of v4, /device:TPU:0, one launch (start us, length us, event | category | flops | bytes accessed | tf_op | source)
XLA Modules:
  0.0 133.9 jit_solution(11074372729979836756)
XLA Ops:
  0.6 131.8 %coupling.1 = (f32[48,4096]{1,0:T(8,128)S(1)}, f32[1,384]{1,0:T(1,128)S(1)}, f32[1,768]{1,0:T(1,128)S(1)}) custom-call(f32[48,4096]{1,0:T(8,128)} %x_hbm.1, f32[48,4096]{1,0:T(8,128)} %y_hbm.1), custom_call_target="tpu_custom_call" | custom-call | tf_op jit(solution)/shard_map/coupling/pallas_call | solution.py:642
  132.4 1.5 %hand_out.1 = (f32[48,4096]{1,0:T(8,128)}, f32[384]{0:T(512)}, f32[768]{0:T(1024)}) custom-call(f32[48,4096]{1,0:T(8,128)S(1)} %get-tuple-element.6.t_in, f32[1,384]{1,0:T(1,128)S(1)} %get-tuple-element.7.f_in, f32[1,768]{1,0:T(1,128)S(1)} %get-tuple-element.8.g_in), custom_call_target="tpu_custom_call" | custom-call | tf_op jit(solution)/shard_map/hand_out/pallas_call | solution.py:657

commit v5 on v4

--- a/solution.py
+++ b/solution.py
@@ -25,8 +25,8 @@
 NSAMP = 6144
 LOGN = math.log(NSAMP)
 SCALE = 1.0 / (WIDTH * EPS)
-CH = 4
-CW = HALF // CH
+CUTS = (0, 256, 512, 1024, 1536, 2048)
+CH = len(CUTS) - 1
 
 
 def split(v):
@@ -276,7 +276,7 @@
         return c
 
     def group3(i, c):
-        own_block(lax.rem(i, 4), i // 4)
+        own_block(i, 0)
         return c
 
     def group4(i, c):
@@ -284,7 +284,7 @@
         return c
 
     def group5(i, c):
-        own_block(2 + i, 1)
+        own_block(i, 1)
         return c
 
     lax.fori_loop(0, 4, group1, 0)
@@ -294,25 +294,31 @@
         got_y(slot(3, "c"), k)
         got_y(slot(2, "b"), k)
     lax.fori_loop(0, 2, group2, 0)
-    lax.fori_loop(0, 6, group3, 0)
+    lax.fori_loop(0, 4, group3, 0)
     for k in range(2):
         got_y(slot(1, "c"), k)
         got_y(slot(2, "c"), k)
         got_y(slot(3, "b"), k)
     lax.fori_loop(0, 2, group4, 0)
-    lax.fori_loop(0, 2, group5, 0)
-
-    def pair_wait(k, c):
-        d = pltpu.make_async_remote_copy(
+    lax.fori_loop(0, 4, group5, 0)
+
+    def pair_wait(i, c):
+        m8, s8 = c
+        hi = (1 - i // 4) * yhi + (i // 4) * (1 - yhi)
+        k = hi * 4 + at_z(lax.rem(3 * i, 4))
+        cp = pltpu.make_async_remote_copy(
             src_ref=ps.at[k], dst_ref=pr.at[k], send_sem=prs.at[0, k], recv_sem=prs.at[1, k], device_id=pa, device_id_type=MESH
         )
-        d.wait_recv()
-        d.wait_send()
+        cp.wait_recv()
+        cp.wait_send()
         at = pl.ds(pl.multiple_of(k * BLK, BLK), BLK)
-        lg[at, :] = lg[at, :] + pr[k]
-        return c
-
-    lax.fori_loop(0, NB, pair_wait, 0)
+        v = lg[at, :] + pr[k]
+        lg[at, :] = v
+        v = v.reshape(12, 8, ROWS)
+        top = jnp.maximum(m8, jnp.max(v, axis=0))
+        return top, s8 * jnp.exp(m8 - top) + jnp.sum(jnp.exp(v - top[None]), axis=0)
+
+    m8, s8 = lax.fori_loop(0, NB, pair_wait, (jnp.full((8, ROWS), -1e30, F32), jnp.zeros((8, ROWS), F32)))
 
     def send_logits(k):
         at = pl.ds(LO_AT[k], LO_AT[k + 1] - LO_AT[k])
@@ -333,7 +339,7 @@
             ).start()
             return c
 
-        lax.fori_loop(1, 8, go_, 0)
+        lax.fori_loop(1, 8, go_, 0, unroll=True)
 
         def done():
             def wt(k, c):
@@ -345,7 +351,7 @@
                 w.wait_recv()
                 return c
 
-            lax.fori_loop(1, 8, wt, 0)
+            lax.fori_loop(1, 8, wt, 0, unroll=True)
             return rx[rnd]
 
         return done
@@ -361,7 +367,7 @@
             ).start()
             return c
 
-        lax.fori_loop(1, 16, go_, 0)
+        lax.fori_loop(1, 16, go_, 0, unroll=True)
 
         def done():
             def wt(k, c):
@@ -372,7 +378,7 @@
                 ).wait_recv()
                 return c
 
-            lax.fori_loop(1, 16, wt, 0)
+            lax.fori_loop(1, 16, wt, 0, unroll=True)
             return buf[rnd]
 
         return done
@@ -384,15 +390,8 @@
     def blk(k):
         return slice(BLK * k, BLK * k + BLK)
 
-    m8 = None
-    for k in range(NB):
-        piece = jnp.max(lg[blk(k), :].reshape(12, 8, ROWS), axis=0)
-        m8 = piece if m8 is None else jnp.maximum(m8, piece)
     m = jnp.max(m8, axis=0, keepdims=True)
-    s8 = jnp.zeros((8, ROWS), F32)
-    for k in range(NB):
-        s8 = s8 + jnp.sum(jnp.exp(lg[blk(k), :] - m).reshape(12, 8, ROWS), axis=0)
-    tot = jnp.sum(s8, axis=0, keepdims=True)
+    tot = jnp.sum(s8 * jnp.exp(m8 - m), axis=0, keepdims=True)
     done = ex_rows(0, row_msg(rows3(m) + rows3(tot)))
     send_logits(0)
     everyone = done()
@@ -406,9 +405,10 @@
     for k in range(NB):
         a = lg[blk(k), :] + f1
         cm = jnp.max(a, axis=1, keepdims=True)
-        ct = jnp.sum(jnp.exp(a - cm), axis=1, keepdims=True)
+        e = jnp.exp(a - cm)
+        q_[blk(k), :] = e
         pm = pm + pack_block(k, cm)
-        pt = pt + pack_block(k, ct)
+        pt = pt + pack_block(k, jnp.sum(e, axis=1, keepdims=True))
     everyone = ex_cols(cx1, cx1s, jnp.concatenate([pm, pt], axis=0), 0)()
     mm = everyone[:, 0:8, :]
     top = jnp.max(mm, axis=0)
@@ -418,9 +418,10 @@
     go[0] = g1
     send(go.at[0], go.at[1], gs.at[0], pa)
 
+    fac = jnp.exp(pm + g1)
     s8 = jnp.zeros((8, ROWS), F32)
     for k in range(NB):
-        p = jnp.exp(lg[blk(k), :] + f1 + unpack(g1, 12 * k, 12))
+        p = q_[blk(k), :] * unpack(fac, 12 * k, 12)
         q_[blk(k), :] = p
         s8 = s8 + jnp.sum(p.reshape(12, 8, ROWS), axis=0)
 
@@ -490,7 +491,10 @@
         )
 
     def cols_of(c):
-        return slice(CW * c, CW * c + CW)
+        return pl.ds(CUTS[c], CUTS[c + 1] - CUTS[c])
+
+    def cut(ref, i, c):
+        return ref.at[i, :, cols_of(c)]
 
     def compute(c):
         t = part(0, own_rows, cols_of(c))
@@ -500,40 +504,54 @@
             wh[1] = hi
             wl[1] = low
         t = t + part(1, far_rows, cols_of(c))
-        tp[c] = t.reshape(8, OWN, CW)
+        tp[:, :, cols_of(c)] = t.reshape(8, OWN, CUTS[c + 1] - CUTS[c])
+
+    def pass_on(i, to, k, c, dev):
+        send(cut(tp, i, c), cut(to, k, c), (r1s if to is r1 else r2s).at[c, k], dev)
+
+    def add(i, k, c):
+        tp[i, :, cols_of(c)] = tp[i, :, cols_of(c)] + r1[k, :, cols_of(c)]
 
     def start_pair(c):
-        send(tp.at[c, xa + at_x(2)], r1.at[c, 0], r1s.at[c, 0], xp)
-        send(tp.at[c, xa + at_x(3)], r2.at[c, 0], r2s.at[c, 0], xm)
+        pass_on(xa + at_x(2), r1, 0, c, xp)
+        pass_on(xa + at_x(3), r2, 0, c, xm)
 
     def pass_pair(c):
-        arrived(r1.at[c, 0], r1s.at[c, 0])
-        tp[c, xa + at_x(1)] = tp[c, xa + at_x(1)] + r1[c, 0]
-        send(tp.at[c, xa + at_x(1)], r2.at[c, 1], r2s.at[c, 1], xp)
+        arrived(cut(r1, 0, c), r1s.at[c, 0])
+        add(xa + at_x(1), 0, c)
+        pass_on(xa + at_x(1), r2, 1, c, xp)
 
     def start_own(c):
-        send(tp.at[c, xo + at_x(2)], r1.at[c, 1], r1s.at[c, 1], xm)
-        send(tp.at[c, xo + at_x(1)], r2.at[c, 3], r2s.at[c, 3], xp)
+        pass_on(xo + at_x(2), r1, 1, c, xm)
+
+    def last_own(c):
+        pass_on(xo + at_x(1), r2, 3, c, xp)
 
     def pass_own(c):
-        arrived(r1.at[c, 1], r1s.at[c, 1])
-        tp[c, xo + at_x(3)] = tp[c, xo + at_x(3)] + r1[c, 1]
-        send(tp.at[c, xo + at_x(3)], r2.at[c, 2], r2s.at[c, 2], xm)
+        arrived(cut(r1, 1, c), r1s.at[c, 1])
+        add(xo + at_x(3), 1, c)
+        pass_on(xo + at_x(3), r2, 2, c, xm)
+
+    def both(i, c, k):
+        for m in (k, k + 1):
+            arrived(cut(r2, m, c), r2s.at[c, m])
+        return tp[i, :, cols_of(c)] + r2[k, :, cols_of(c)] + r2[k + 1, :, cols_of(c)]
 
     def final_pair(c):
-        arrived(r2.at[c, 0], r2s.at[c, 0])
-        arrived(r2.at[c, 1], r2s.at[c, 1])
-        tp[c, xa + x] = tp[c, xa + x] + r2[c, 0] + r2[c, 1]
-        send(tp.at[c, xa + x], pf.at[c], pfs.at[c], pa)
+        tp[xa + x, :, cols_of(c)] = both(xa + x, c, 0)
+        send(cut(tp, xa + x, c), pf.at[:, cols_of(c)], pfs.at[c], pa)
 
     for c in range(CH):
         compute(c)
         start_pair(c)
+        start_own(c)
         if c:
             pass_pair(c - 1)
+        else:
+            last_own(c)
     pass_pair(CH - 1)
-    for c in range(CH):
-        start_own(c)
+    for c in range(1, CH):
+        last_own(c)
 
     fin = flat3(jnp.sum(total()[:, 0:3, :], axis=0))
     lane = lax.broadcasted_iota(jnp.int32, (OWN, ROWS), 1)
@@ -549,13 +567,12 @@
             pass_own(c - 1)
     pass_own(CH - 1)
     for c in range(CH):
-        arrived(r2.at[c, 2], r2s.at[c, 2])
-        arrived(r2.at[c, 3], r2s.at[c, 3])
-        t = tp[c, xo + x] + r2[c, 2] + r2[c, 3]
-        t_out[:, pl.ds(pl.multiple_of(h * HALF + c * CW, CW), CW)] = t * norm
+        width = CUTS[c + 1] - CUTS[c]
+        t_out[:, pl.ds(pl.multiple_of(h * HALF + CUTS[c], 256), width)] = both(xo + x, c, 2) * norm
     for c in range(CH):
-        arrived(pf.at[c], pfs.at[c])
-        t_out[:, pl.ds(pl.multiple_of((1 - h) * HALF + c * CW, CW), CW)] = pf[c] * norm
+        width = CUTS[c + 1] - CUTS[c]
+        arrived(pf.at[:, cols_of(c)], pfs.at[c])
+        t_out[:, pl.ds(pl.multiple_of((1 - h) * HALF + CUTS[c], 256), width)] = pf[:, cols_of(c)] * norm
 
     for cp in sent:
         cp.wait_send()
@@ -615,10 +632,10 @@
         vm((ROWS, COLS), F32),
         vm((2, ROWS, COLS), BF16),
         vm((2, ROWS, COLS), BF16),
-        vm((CH, 8, OWN, CW), F32),
-        vm((CH, 2, OWN, CW), F32),
-        vm((CH, 4, OWN, CW), F32),
-        vm((CH, OWN, CW), F32),
+        vm((8, OWN, HALF), F32),
+        vm((2, OWN, HALF), F32),
+        vm((4, OWN, HALF), F32),
+        vm((OWN, HALF), F32),
         vm((4, 8, 8, 128), F32),
         vm((1, 16, 16, 128), F32),
         vm((2, 16, 8, 128), F32),

time: 135 us -> 130 us (0.963)
  Pallas kernels: 133 us -> 129 us
    pallas_call x1, Pallas kernels: 132 us -> 127 us  [body(): pl.pallas_call(kernel, out_shape=(vm((OWN, WIDTH), F32), vm((1, ROWS), F3...]
where the time goes in v5:
time: 130 us; the launch traced here: 129 us
  Pallas kernels  129 us (99%)
    pallas_call x1, Pallas kernels, body(): pl.pallas_call(kernel, out_shape=(vm((OWN, WIDTH), F32), vm((1, ROWS), F3...  127 us

profile of v5, /device:TPU:0, one launch (start us, length us, event | category | flops | bytes accessed | tf_op | source)
XLA Modules:
  0.0 129.4 jit_solution(2178927206392826579)
XLA Ops:
  0.6 127.1 %coupling.1 = (f32[48,4096]{1,0:T(8,128)S(1)}, f32[1,384]{1,0:T(1,128)S(1)}, f32[1,768]{1,0:T(1,128)S(1)}) custom-call(f32[48,4096]{1,0:T(8,128)} %x_hbm.1, f32[48,4096]{1,0:T(8,128)} %y_hbm.1), custom_call_target="tpu_custom_call" | custom-call | tf_op jit(solution)/shard_map/coupling/pallas_call | solution.py:659
  127.8 1.5 %hand_out.1 = (f32[48,4096]{1,0:T(8,128)}, f32[384]{0:T(512)}, f32[768]{0:T(1024)}) custom-call(f32[48,4096]{1,0:T(8,128)S(1)} %get-tuple-element.6.t_in, f32[1,384]{1,0:T(1,128)S(1)} %get-tuple-element.7.f_in, f32[1,768]{1,0:T(1,128)S(1)} %get-tuple-element.8.g_in), custom_call_target="tpu_custom_call" | custom-call | tf_op jit(solution)/shard_map/hand_out/pallas_call | solution.py:674

commit v6 on v5

--- a/solution.py
+++ b/solution.py
@@ -21,7 +21,7 @@
 BLK = 96
 NB = COLS // BLK
 PIECE = OWN // 2
-LO_AT = (0, 320, 576, 768)
+LO_AT = (0, 256, 496, 672, 768)
 NSAMP = 6144
 LOGN = math.log(NSAMP)
 SCALE = 1.0 / (WIDTH * EPS)
@@ -78,7 +78,7 @@
     x_hbm, y_hbm, t_out, f_out, g_out,
     xb, yb, xh, xl, yh_, yl_, xs, rsq, ps, pr, lg, lo, q_, pn, po, wh, wl, tp, r1, r2, pf,
     rx, cx1, cx, go, vo,
-    loc, xr, yr, yr2, prs, lsem, rxs, cx1s, cxs, gs, r1s, r2s, pfs, ssem,
+    loc, xr, yr, yr2, prs, los, lsem, rxs, cx1s, cxs, gs, r1s, r2s, pfs, asem, tsem,
 ):
     n = lax.axis_index("noise")
     d = lax.axis_index("dp")
@@ -131,33 +131,36 @@
         pl.semaphore_signal(barrier, inc=1, device_id=dev, device_id_type=MESH)
     pl.semaphore_wait(barrier, 7)
 
-    sent = []
-
-    def send(src, dst, rsem, dev):
-        c = pltpu.make_async_remote_copy(
-            src_ref=src, dst_ref=dst, send_sem=ssem.at[len(sent)], recv_sem=rsem, device_id=dev, device_id_type=MESH
-        )
-        c.start()
-        sent.append(c)
-        return c
+    def send(src, dst, rsem, dev, ssend):
+        pltpu.make_async_remote_copy(
+            src_ref=src, dst_ref=dst, send_sem=ssend, recv_sem=rsem, device_id=dev, device_id_type=MESH
+        ).start()
+
+    def all_sent(ref, ssend):
+        pltpu.make_async_remote_copy(
+            src_ref=ref, dst_ref=ref, send_sem=ssend, recv_sem=lsem.at[0], device_id=sib, device_id_type=MESH
+        ).wait_send()
+
+    PA, PB, ZP, ZM, XP, XM, SIB = range(7)
+    TO = [pa, pb, zp, zm, xp, xm, sib]
 
     def arrived(dst, rsem):
         pltpu.make_async_remote_copy(
-            src_ref=dst, dst_ref=dst, send_sem=ssem.at[0], recv_sem=rsem, device_id=sib, device_id_type=MESH
+            src_ref=dst, dst_ref=dst, send_sem=asem.at[0], recv_sem=rsem, device_id=sib, device_id_type=MESH
         ).wait_recv()
 
-    def send_y(s, k, dev):
-        send(yb.at[s, core, k], yb.at[s, core, k], yr.at[s, k], dev)
+    def send_y(s, k, to):
+        send(yb.at[s, core, k], yb.at[s, core, k], yr.at[s, k], TO[to], asem.at[to])
 
     def cross_y(s, k):
-        send(yb.at[s, core, k], yb.at[s, core, k], yr2.at[s, k], sib)
+        send(yb.at[s, core, k], yb.at[s, core, k], yr2.at[s], sib, asem.at[SIB])
 
     def got_y(s, k):
         arrived(yb.at[s, core, k], yr.at[s, k])
         cross_y(s, k)
 
-    def send_x(i, k, dev):
-        send(xb.at[i, k], xb.at[i, k], xr.at[i, k], dev)
+    def send_x(i, k, to):
+        send(xb.at[i, k], xb.at[i, k], xr.at[i, k], TO[to], asem.at[to])
 
     def got_x(i, k):
         arrived(xb.at[i, k], xr.at[i, k])
@@ -179,8 +182,7 @@
         return c
 
     def split_y(s):
-        for k in range(2):
-            arrived(yb.at[s, 1 - core, k], yr2.at[s, k])
+        arrived(yb.at[s, 1 - core], yr2.at[s])
         v = yb[s].reshape(BLK, HALF)
         hi, low = split(v)
         at = pl.ds(pl.multiple_of(s * BLK, BLK), BLK)
@@ -189,60 +191,60 @@
         return hi, low, jnp.sum(v * v, axis=1, keepdims=True)
 
     for k in range(2):
-        send(x_hbm.at[pl.ds(k * PIECE, PIECE), kother], xb.at[d, k], xr.at[d, k], pa)
+        send(x_hbm.at[pl.ds(k * PIECE, PIECE), kother], xb.at[d, k], xr.at[d, k], pa, asem.at[PA])
     for k in range(2):
         mine = slot(0, "o")
-        send(y_hbm.at[pl.ds(k * PIECE, PIECE), kother], yb.at[mine, core, k], yr.at[mine, k], pa)
+        send(y_hbm.at[pl.ds(k * PIECE, PIECE), kother], yb.at[mine, core, k], yr.at[mine, k], pa, asem.at[PA])
     for k in range(2):
         cx_own[k].wait()
-        send_x(d, k, xp)
-        send_x(d, k, xm)
+        send_x(d, k, XP)
+        send_x(d, k, XM)
         cy_own[k].wait()
-        send_y(mine, k, zp)
-        send_y(mine, k, zm)
-        send_y(mine, k, pb)
+        send_y(mine, k, ZP)
+        send_y(mine, k, ZM)
+        send_y(mine, k, PB)
         cross_y(mine, k)
 
     for k in range(2):
         got_x(xa + x, k)
-        send_x(xa + x, k, xp)
-        send_x(xa + x, k, xm)
+        send_x(xa + x, k, XP)
+        send_x(xa + x, k, XM)
         got_y(slot(3, "o"), k)
-        send_y(slot(3, "o"), k, zp)
+        send_y(slot(3, "o"), k, ZP)
         got_y(slot(0, "b"), k)
-        send_y(slot(0, "b"), k, zm)
+        send_y(slot(0, "b"), k, ZM)
         got_y(slot(1, "o"), k)
         got_x(xo + at_x(1), k)
         got_x(xo + at_x(3), k)
-        send_x(xo + at_x(3), k, xp)
+        send_x(xo + at_x(3), k, XP)
 
     lax.fori_loop(0, 1, split_xs, 0)
 
     for k in range(2):
         got_y(slot(0, "a"), k)
-        send_y(slot(0, "a"), k, zp)
-        send_y(slot(0, "a"), k, zm)
-        send_y(slot(0, "a"), k, pb)
+        send_y(slot(0, "a"), k, ZP)
+        send_y(slot(0, "a"), k, ZM)
+        send_y(slot(0, "a"), k, PB)
         got_x(xa + at_x(1), k)
-        send_x(xa + at_x(1), k, xm)
+        send_x(xa + at_x(1), k, XM)
         got_x(xa + at_x(3), k)
         got_y(slot(2, "o"), k)
         got_y(slot(1, "b"), k)
     for k in range(2):
-        send_y(slot(2, "o"), k, pb)
+        send_y(slot(2, "o"), k, PB)
     lax.fori_loop(0, 2, lambda i, c: split_xs(1 + 2 * i, c), 0)
 
     for k in range(2):
         got_y(slot(0, "c"), k)
-        send_y(slot(0, "c"), k, zp)
+        send_y(slot(0, "c"), k, ZP)
         got_y(slot(1, "a"), k)
-        send_y(slot(1, "a"), k, zm)
+        send_y(slot(1, "a"), k, ZM)
         got_y(slot(3, "a"), k)
         got_x(xo + at_x(2), k)
         got_x(xa + at_x(2), k)
     for k in range(2):
-        send_y(slot(0, "b"), k, zp)
-        send_y(slot(0, "c"), k, zm)
+        send_y(slot(0, "b"), k, ZP)
+        send_y(slot(0, "c"), k, ZM)
     lax.fori_loop(2, 3, split_xs, 0)
     r = lax.broadcasted_iota(jnp.int32, (128, 128), 0)
     c = lax.broadcasted_iota(jnp.int32, (128, 128), 1)
@@ -260,7 +262,7 @@
         k = (is_c * (1 - yhi) + (1 - is_c) * yhi) * 4 + at_z(dz)
         ps[k] = block((1 - h) * 8 + k)
         pltpu.make_async_remote_copy(
-            src_ref=ps.at[k], dst_ref=pr.at[k], send_sem=prs.at[0, k], recv_sem=prs.at[1, k], device_id=pa, device_id_type=MESH
+            src_ref=ps.at[k], dst_ref=pr.at[k], send_sem=lsem.at[1], recv_sem=prs.at[k], device_id=pa, device_id_type=MESH
         ).start()
 
     def own_block(dz, is_b):
@@ -290,7 +292,7 @@
     lax.fori_loop(0, 4, group1, 0)
     for k in range(2):
         got_y(slot(2, "a"), k)
-        send_y(slot(2, "a"), k, pb)
+        send_y(slot(2, "a"), k, PB)
         got_y(slot(3, "c"), k)
         got_y(slot(2, "b"), k)
     lax.fori_loop(0, 2, group2, 0)
@@ -306,11 +308,7 @@
         m8, s8 = c
         hi = (1 - i // 4) * yhi + (i // 4) * (1 - yhi)
         k = hi * 4 + at_z(lax.rem(3 * i, 4))
-        cp = pltpu.make_async_remote_copy(
-            src_ref=ps.at[k], dst_ref=pr.at[k], send_sem=prs.at[0, k], recv_sem=prs.at[1, k], device_id=pa, device_id_type=MESH
-        )
-        cp.wait_recv()
-        cp.wait_send()
+        arrived(pr.at[k], prs.at[k])
         at = pl.ds(pl.multiple_of(k * BLK, BLK), BLK)
         v = lg[at, :] + pr[k]
         lg[at, :] = v
@@ -322,66 +320,41 @@
 
     def send_logits(k):
         at = pl.ds(LO_AT[k], LO_AT[k + 1] - LO_AT[k])
-        send(lg.at[at], lo.at[at], lsem.at[k], pa)
+        send(lg.at[at], lo.at[at], los.at[k], pa, lsem.at[2])
 
     def got_logits(k):
         at = pl.ds(LO_AT[k], LO_AT[k + 1] - LO_AT[k])
-        arrived(lo.at[at], lsem.at[k])
+        arrived(lo.at[at], los.at[k])
+
+    def exchange(buf, sems, rnd, mine, peers, msg):
+        buf[rnd, mine] = msg
+        for dev in peers:
+            pltpu.make_async_remote_copy(
+                src_ref=buf.at[rnd, mine], dst_ref=buf.at[rnd, mine], send_sem=sems.at[0, rnd], recv_sem=sems.at[1, rnd],
+                device_id=dev, device_id_type=MESH,
+            ).start()
+        every = buf.at[rnd, pl.ds(0, len(peers))]
+        all_of = pltpu.make_async_remote_copy(
+            src_ref=every, dst_ref=every, send_sem=sems.at[0, rnd], recv_sem=sems.at[1, rnd],
+            device_id=peers[0], device_id_type=MESH,
+        )
+        small.append(all_of)
+
+        def done():
+            all_of.wait_recv()
+            return buf[rnd]
+
+        return done
+
+    small = []
+    row_peers = [(n, lax.rem(d + k, 8)) for k in range(1, 8)]
+    col_peers = [col_dev(lax.rem(n + k, 16)) for k in range(1, 16)]
 
     def ex_rows(rnd, msg):
-        rx[rnd, d] = msg
-
-        def go_(k, c):
-            p = lax.rem(d + k, 8)
-            pltpu.make_async_remote_copy(
-                src_ref=rx.at[rnd, d], dst_ref=rx.at[rnd, d], send_sem=rxs.at[0, rnd, p], recv_sem=rxs.at[1, rnd, d],
-                device_id=(n, p), device_id_type=MESH,
-            ).start()
-            return c
-
-        lax.fori_loop(1, 8, go_, 0, unroll=True)
-
-        def done():
-            def wt(k, c):
-                p = lax.rem(d + k, 8)
-                w = pltpu.make_async_remote_copy(
-                    src_ref=rx.at[rnd, p], dst_ref=rx.at[rnd, p], send_sem=rxs.at[0, rnd, p], recv_sem=rxs.at[1, rnd, p],
-                    device_id=(n, p), device_id_type=MESH,
-                )
-                w.wait_recv()
-                return c
-
-            lax.fori_loop(1, 8, wt, 0, unroll=True)
-            return rx[rnd]
-
-        return done
-
-    def ex_cols(buf, sem, msg, rnd):
-        buf[rnd, n] = msg
-
-        def go_(k, c):
-            p = lax.rem(n + k, 16)
-            pltpu.make_async_remote_copy(
-                src_ref=buf.at[rnd, n], dst_ref=buf.at[rnd, n], send_sem=sem.at[0, rnd, p], recv_sem=sem.at[1, rnd, n],
-                device_id=col_dev(p), device_id_type=MESH,
-            ).start()
-            return c
-
-        lax.fori_loop(1, 16, go_, 0, unroll=True)
-
-        def done():
-            def wt(k, c):
-                p = lax.rem(n + k, 16)
-                pltpu.make_async_remote_copy(
-                    src_ref=buf.at[rnd, p], dst_ref=buf.at[rnd, p], send_sem=sem.at[0, rnd, p], recv_sem=sem.at[1, rnd, p],
-                    device_id=col_dev(p), device_id_type=MESH,
-                ).wait_recv()
-                return c
-
-            lax.fori_loop(1, 16, wt, 0, unroll=True)
-            return buf[rnd]
-
-        return done
+        return exchange(rx, rxs, rnd, d, row_peers, msg)
+
+    def ex_cols(buf, sems, msg, rnd):
+        return exchange(buf, sems, rnd, n, col_peers, msg)
 
     def row_msg(parts):
         parts = parts + [jnp.zeros((1, 128), F32)] * (8 - len(parts))
@@ -409,14 +382,26 @@
         q_[blk(k), :] = e
         pm = pm + pack_block(k, cm)
         pt = pt + pack_block(k, jnp.sum(e, axis=1, keepdims=True))
-    everyone = ex_cols(cx1, cx1s, jnp.concatenate([pm, pt], axis=0), 0)()
+    done = ex_cols(cx1, cx1s, jnp.concatenate([pm, pt], axis=0), 0)
+    for ref, to in (
+        (xb.at[pl.ds(0, 2)], PA),
+        (yb.at[pl.ds(0, 4), core], PB),
+        (yb.at[pl.ds(0, 5), core], ZP),
+        (yb.at[pl.ds(0, 5), core], ZM),
+        (xb.at[pl.ds(0, 3)], XP),
+        (xb.at[pl.ds(0, 3)], XM),
+        (yb.at[:, core], SIB),
+    ):
+        all_sent(ref, asem.at[to])
+    all_sent(ps, lsem.at[1])
+    everyone = done()
     mm = everyone[:, 0:8, :]
     top = jnp.max(mm, axis=0)
     tt = jnp.sum(everyone[:, 8:16, :] * jnp.exp(mm - top[None]), axis=0)
     used = lax.broadcasted_iota(jnp.int32, (8, 128), 1) < 96
     g1 = jnp.where(used, LOGN - top - jnp.log(jnp.where(used, tt, 1.0)), 0.0)
     go[0] = g1
-    send(go.at[0], go.at[1], gs.at[0], pa)
+    send(go.at[0], go.at[1], gs.at[0], pa, lsem.at[3])
 
     fac = jnp.exp(pm + g1)
     s8 = jnp.zeros((8, ROWS), F32)
@@ -465,17 +450,20 @@
         far(range(0, 2))
 
     def in_col2():
+        send_logits(3)
         got_logits(1)
-        far(range(2, 4))
+        far(range(2, 3))
         got_logits(2)
-        far(range(4, 6))
+        far(range(3, 5))
+        got_logits(3)
+        far(range(5, 6))
 
     u = row_step(1, s8, in_row1)
     v = col_step(0, u, lambda: turn(q_, pn, range(3, 6)))
     u = row_step(2, row_sums(v), in_row2)
     v = col_step(1, u, in_col2)
     vo[0] = v
-    send(vo.at[0], vo.at[1], gs.at[1], pa)
+    send(vo.at[0], vo.at[1], gs.at[1], pa, lsem.at[4])
     total = ex_rows(3, row_msg(rows3(jnp.sum(row_sums(v), axis=0, keepdims=True))))
 
     hi, low = split(pn[...] * packed_row(v))
@@ -506,40 +494,40 @@
         t = t + part(1, far_rows, cols_of(c))
         tp[:, :, cols_of(c)] = t.reshape(8, OWN, CUTS[c + 1] - CUTS[c])
 
-    def pass_on(i, to, k, c, dev):
-        send(cut(tp, i, c), cut(to, k, c), (r1s if to is r1 else r2s).at[c, k], dev)
+    def pass_on(i, buf, k, c, to):
+        sem = r1s.at[c, k] if buf is r1 else r2s.at[c, k // 2]
+        send(cut(tp, i, c), cut(buf, k, c), sem, TO[to], tsem.at[to])
 
     def add(i, k, c):
         tp[i, :, cols_of(c)] = tp[i, :, cols_of(c)] + r1[k, :, cols_of(c)]
 
     def start_pair(c):
-        pass_on(xa + at_x(2), r1, 0, c, xp)
-        pass_on(xa + at_x(3), r2, 0, c, xm)
+        pass_on(xa + at_x(2), r1, 0, c, XP)
+        pass_on(xa + at_x(3), r2, 0, c, XM)
 
     def pass_pair(c):
         arrived(cut(r1, 0, c), r1s.at[c, 0])
         add(xa + at_x(1), 0, c)
-        pass_on(xa + at_x(1), r2, 1, c, xp)
+        pass_on(xa + at_x(1), r2, 1, c, XP)
 
     def start_own(c):
-        pass_on(xo + at_x(2), r1, 1, c, xm)
+        pass_on(xo + at_x(2), r1, 1, c, XM)
 
     def last_own(c):
-        pass_on(xo + at_x(1), r2, 3, c, xp)
+        pass_on(xo + at_x(1), r2, 3, c, XP)
 
     def pass_own(c):
         arrived(cut(r1, 1, c), r1s.at[c, 1])
         add(xo + at_x(3), 1, c)
-        pass_on(xo + at_x(3), r2, 2, c, xm)
+        pass_on(xo + at_x(3), r2, 2, c, XM)
 
     def both(i, c, k):
-        for m in (k, k + 1):
-            arrived(cut(r2, m, c), r2s.at[c, m])
+        arrived(r2.at[pl.ds(k, 2), :, cols_of(c)], r2s.at[c, k // 2])
         return tp[i, :, cols_of(c)] + r2[k, :, cols_of(c)] + r2[k + 1, :, cols_of(c)]
 
     def final_pair(c):
         tp[xa + x, :, cols_of(c)] = both(xa + x, c, 0)
-        send(cut(tp, xa + x, c), pf.at[:, cols_of(c)], pfs.at[c], pa)
+        send(cut(tp, xa + x, c), pf.at[:, cols_of(c)], pfs, pa, tsem.at[PA])
 
     for c in range(CH):
         compute(c)
@@ -569,34 +557,17 @@
     for c in range(CH):
         width = CUTS[c + 1] - CUTS[c]
         t_out[:, pl.ds(pl.multiple_of(h * HALF + CUTS[c], 256), width)] = both(xo + x, c, 2) * norm
-    for c in range(CH):
-        width = CUTS[c + 1] - CUTS[c]
-        arrived(pf.at[:, cols_of(c)], pfs.at[c])
-        t_out[:, pl.ds(pl.multiple_of((1 - h) * HALF + CUTS[c], 256), width)] = pf[:, cols_of(c)] * norm
-
-    for cp in sent:
+    arrived(pf, pfs)
+    t_out[:, kother] = pf[...] * norm
+
+    all_sent(lg, lsem.at[2])
+    all_sent(go.at[0], lsem.at[3])
+    all_sent(vo.at[0], lsem.at[4])
+    all_sent(pf, tsem.at[PA])
+    for to in (XP, XM):
+        all_sent(tp.at[pl.ds(0, 3)], tsem.at[to])
+    for cp in small:
         cp.wait_send()
-
-    def drain_rows(k, c):
-        p = lax.rem(d + k, 8)
-        for rnd in range(4):
-            pltpu.make_async_remote_copy(
-                src_ref=rx.at[rnd, d], dst_ref=rx.at[rnd, d], send_sem=rxs.at[0, rnd, p], recv_sem=rxs.at[1, rnd, d],
-                device_id=(n, p), device_id_type=MESH,
-            ).wait_send()
-        return c
-
-    def drain_cols(k, c):
-        p = lax.rem(n + k, 16)
-        for buf, sem, rnd in ((cx1, cx1s, 0), (cx, cxs, 0), (cx, cxs, 1)):
-            pltpu.make_async_remote_copy(
-                src_ref=buf.at[rnd, n], dst_ref=buf.at[rnd, n], send_sem=sem.at[0, rnd, p], recv_sem=sem.at[1, rnd, n],
-                device_id=col_dev(p), device_id_type=MESH,
-            ).wait_send()
-        return c
-
-    lax.fori_loop(1, 8, drain_rows, 0)
-    lax.fori_loop(1, 16, drain_cols, 0)
 
 
 def hand_out(t_in, f_in, g_in, t_out, f_out, g_out, sem):
@@ -644,17 +615,19 @@
         dma((2, 2)),
         dma((8, 2)),
         dma((16, 2)),
-        dma((16, 2)),
-        dma((2, NB)),
-        dma((3,)),
-        dma((2, 4, 8)),
-        dma((2, 1, 16)),
-        dma((2, 2, 16)),
+        dma((16,)),
+        dma((NB,)),
+        dma((4,)),
+        dma((5,)),
+        dma((2, 4)),
+        dma((2, 1)),
+        dma((2, 2)),
         dma((2,)),
         dma((CH, 2)),
-        dma((CH, 4)),
-        dma((CH,)),
-        dma((192,)),
+        dma((CH, 2)),
+        dma,
+        dma((7,)),
+        dma((7,)),
     ]
     t, f, g = pl.pallas_call(
         kernel,

time: 130 us -> 127 us (0.977)
  Pallas kernels: 129 us -> 126 us
    pallas_call x1, Pallas kernels: 127 us -> 125 us  [body(): pl.pallas_call(kernel, out_shape=(vm((OWN, WIDTH), F32), vm((1, ROWS), F3...]
where the time goes in v6:
time: 127 us
  Pallas kernels  126 us (99%)
    pallas_call x1, Pallas kernels, body(): pl.pallas_call(kernel, out_shape=(vm((OWN, WIDTH), F32), vm((1, ROWS), F3...  125 us

profile of v6, /device:TPU:0, one launch (start us, length us, event | category | flops | bytes accessed | tf_op | source)
XLA Modules:
  0.0 127.1 jit_solution(13445284004558557057)
XLA Ops:
  0.6 124.8 %coupling.1 = (f32[48,4096]{1,0:T(8,128)S(1)}, f32[1,384]{1,0:T(1,128)S(1)}, f32[1,768]{1,0:T(1,128)S(1)}) custom-call(f32[48,4096]{1,0:T(8,128)} %x_hbm.1, f32[48,4096]{1,0:T(8,128)} %y_hbm.1), custom_call_target="tpu_custom_call" | custom-call | tf_op jit(solution)/shard_map/coupling/pallas_call | solution.py:632
  125.5 1.5 %hand_out.1 = (f32[48,4096]{1,0:T(8,128)}, f32[384]{0:T(512)}, f32[768]{0:T(1024)}) custom-call(f32[48,4096]{1,0:T(8,128)S(1)} %get-tuple-element.6.t_in, f32[1,384]{1,0:T(1,128)S(1)} %get-tuple-element.7.f_in, f32[1,768]{1,0:T(1,128)S(1)} %get-tuple-element.8.g_in), custom_call_target="tpu_custom_call" | custom-call | tf_op jit(solution)/shard_map/hand_out/pallas_call | solution.py:647

commit v7 on v6

--- a/solution.py
+++ b/solution.py
@@ -76,7 +76,7 @@
 
 def kernel(
     x_hbm, y_hbm, t_out, f_out, g_out,
-    xb, yb, xh, xl, yh_, yl_, xs, rsq, ps, pr, lg, lo, q_, pn, po, wh, wl, tp, r1, r2, pf,
+    xb, yb, xh, xl, yh_, yl_, xs, cse, rsq, ps, pr, lg, lo, q_, pn, po, wh, wl, tp, r1, r2, pf,
     rx, cx1, cx, go, vo,
     loc, xr, yr, yr2, prs, los, lsem, rxs, cx1s, cxs, gs, r1s, r2s, pfs, asem, tsem,
 ):
@@ -176,10 +176,11 @@
         xl[at, :] = low
         xs[at, :] = jnp.broadcast_to(jnp.sum(v * v, axis=1, keepdims=True), (OWN, 128))
 
-    def split_xs(i, c):
-        split_x(at_x(i))
-        split_x(4 + at_x(i))
-        return c
+    def fill_rsq(at):
+        r = lax.broadcasted_iota(jnp.int32, (128, 128), 0)
+        c = lax.broadcasted_iota(jnp.int32, (128, 128), 1)
+        piece = jnp.sum(jnp.where(r == c, xs[at, :], 0.0), axis=0, keepdims=True)
+        rsq[:, at] = jnp.broadcast_to(piece, (8, 128))
 
     def split_y(s):
         arrived(yb.at[s, 1 - core], yr2.at[s])
@@ -207,18 +208,23 @@
 
     for k in range(2):
         got_x(xa + x, k)
-        send_x(xa + x, k, XP)
         send_x(xa + x, k, XM)
+        got_x(xo + at_x(3), k)
+        send_x(xo + at_x(3), k, XP)
         got_y(slot(3, "o"), k)
         send_y(slot(3, "o"), k, ZP)
         got_y(slot(0, "b"), k)
         send_y(slot(0, "b"), k, ZM)
         got_y(slot(1, "o"), k)
         got_x(xo + at_x(1), k)
-        got_x(xo + at_x(3), k)
-        send_x(xo + at_x(3), k, XP)
-
-    lax.fori_loop(0, 1, split_xs, 0)
+    for k in range(2):
+        send_x(xa + x, k, XP)
+
+    def split_first(i, c):
+        split_x(lax.rem(i // 3 + ylo, 2) * 4 + at_x(lax.rem(i + i // 2, 4) * (1 - i // 3)))
+        return c
+
+    lax.fori_loop(0, 4, split_first, 0)
 
     for k in range(2):
         got_y(slot(0, "a"), k)
@@ -227,50 +233,85 @@
         send_y(slot(0, "a"), k, PB)
         got_x(xa + at_x(1), k)
         send_x(xa + at_x(1), k, XM)
-        got_x(xa + at_x(3), k)
+        got_x(xo + at_x(2), k)
         got_y(slot(2, "o"), k)
         got_y(slot(1, "b"), k)
     for k in range(2):
         send_y(slot(2, "o"), k, PB)
-    lax.fori_loop(0, 2, lambda i, c: split_xs(1 + 2 * i, c), 0)
+
+    def split_second(i, c):
+        split_x(lax.rem(i + ylo, 2) * 4 + at_x(2 - i))
+        return c
+
+    lax.fori_loop(0, 2, split_second, 0)
+
+    first = pl.ds(pl.multiple_of(256 * ylo, 128), 128)
+    rest = pl.ds(pl.multiple_of(128 * (1 - ylo), 128), 256)
+    fill_rsq(first)
+
+    def pair_send(k, lanes):
+        at = (k,) if lanes is None else (k, slice(None), lanes)
+        pltpu.make_async_remote_copy(
+            src_ref=ps.at[at], dst_ref=pr.at[at], send_sem=lsem.at[1], recv_sem=prs.at[k], device_id=pa, device_id_type=MESH
+        ).start()
+
+    def cross_part(hi, low, csq, lanes):
+        both = dot_nt(jnp.concatenate([hi, low], axis=0), xh[lanes, :])
+        cross = both[:BLK] + both[BLK:] + dot_nt(hi, xl[lanes, :])
+        return (2.0 * cross - csq - rsq[0:1, lanes]) * SCALE
+
+    def pair_first(e, k):
+        hi, low, csq = split_y((1 - h) * 8 + k)
+        cse[e] = jnp.broadcast_to(csq, (BLK, 128))
+        ps[k, :, first] = cross_part(hi, low, csq, first)
+        pair_send(k, first)
+
+    def pair_rest(e, k):
+        at = pl.ds(pl.multiple_of(((1 - h) * 8 + k) * BLK, BLK), BLK)
+        ps[k, :, rest] = cross_part(yh_[at, :], yl_[at, :], cse[e, :, 0:1], rest)
+        pair_send(k, rest)
+
+    ka = yhi * 4 + z
+    kc = (1 - yhi) * 4 + z
+    pair_first(0, ka)
 
     for k in range(2):
         got_y(slot(0, "c"), k)
         send_y(slot(0, "c"), k, ZP)
+        if k:
+            pair_first(1, kc)
         got_y(slot(1, "a"), k)
         send_y(slot(1, "a"), k, ZM)
         got_y(slot(3, "a"), k)
-        got_x(xo + at_x(2), k)
+        got_x(xa + at_x(3), k)
         got_x(xa + at_x(2), k)
     for k in range(2):
         send_y(slot(0, "b"), k, ZP)
         send_y(slot(0, "c"), k, ZM)
-    lax.fori_loop(2, 3, split_xs, 0)
-    r = lax.broadcasted_iota(jnp.int32, (128, 128), 0)
-    c = lax.broadcasted_iota(jnp.int32, (128, 128), 1)
+
+    def split_third(i, c):
+        split_x(xa + at_x(2 + i))
+        return c
+
+    lax.fori_loop(0, 2, split_third, 0)
     for i in range(3):
-        piece = jnp.sum(jnp.where(r == c, xs[128 * i : 128 * i + 128, :], 0.0), axis=0, keepdims=True)
-        rsq[:, 128 * i : 128 * i + 128] = jnp.broadcast_to(piece, (8, 128))
+        fill_rsq(pl.ds(128 * i, 128))
 
     def block(s):
         hi, low, csq = split_y(s)
-        both = dot_nt(jnp.concatenate([hi, low], axis=0), xh[...])
-        cross = both[:BLK] + both[BLK:] + dot_nt(hi, xl[...])
-        return (2.0 * cross - csq - rsq[0:1, :]) * SCALE
+        return cross_part(hi, low, csq, slice(None))
 
     def pair_block(dz, is_c):
         k = (is_c * (1 - yhi) + (1 - is_c) * yhi) * 4 + at_z(dz)
         ps[k] = block((1 - h) * 8 + k)
-        pltpu.make_async_remote_copy(
-            src_ref=ps.at[k], dst_ref=pr.at[k], send_sem=lsem.at[1], recv_sem=prs.at[k], device_id=pa, device_id_type=MESH
-        ).start()
+        pair_send(k, None)
 
     def own_block(dz, is_b):
         k = (is_b * (1 - yhi) + (1 - is_b) * yhi) * 4 + at_z(dz)
         lg[pl.ds(pl.multiple_of(k * BLK, BLK), BLK), :] = block(h * 8 + k)
 
     def group1(i, c):
-        pair_block(lax.rem(i, 2) + 2 * (i // 3), lax.rem(i // 2 + i // 3, 2))
+        pair_block(1 + 2 * i, 0)
         return c
 
     def group2(i, c):
@@ -289,7 +330,9 @@
         own_block(i, 1)
         return c
 
-    lax.fori_loop(0, 4, group1, 0)
+    pair_rest(0, ka)
+    pair_rest(1, kc)
+    lax.fori_loop(0, 2, group1, 0)
     for k in range(2):
         got_y(slot(2, "a"), k)
         send_y(slot(2, "a"), k, PB)
@@ -593,6 +636,7 @@
         vm((2 * COLS, HALF), BF16),
         vm((2 * COLS, HALF), BF16),
         vm((ROWS, 128), F32),
+        vm((2, BLK, 128), F32),
         vm((8, ROWS), F32),
         vm((NB, BLK, ROWS), F32),
         vm((NB, BLK, ROWS), F32),

time: 127 us -> 127 us (level)
  no operation moved by 1% of the time
where the time goes in v7:
time: 127 us
  Pallas kernels  126 us (99%)
    pallas_call x1, Pallas kernels, body(): pl.pallas_call(kernel, out_shape=(vm((OWN, WIDTH), F32), vm((1, ROWS), F3...  124 us

profile of v7, /device:TPU:0, one launch (start us, length us, event | category | flops | bytes accessed | tf_op | source)
XLA Modules:
  0.0 126.6 jit_solution(916618393324033385)
XLA Ops:
  0.6 124.3 %coupling.1 = (f32[48,4096]{1,0:T(8,128)S(1)}, f32[1,384]{1,0:T(1,128)S(1)}, f32[1,768]{1,0:T(1,128)S(1)}) custom-call(f32[48,4096]{1,0:T(8,128)} %x_hbm.1, f32[48,4096]{1,0:T(8,128)} %y_hbm.1), custom_call_target="tpu_custom_call" | custom-call | tf_op jit(solution)/shard_map/coupling/pallas_call | solution.py:676
  124.9 1.5 %hand_out.1 = (f32[48,4096]{1,0:T(8,128)}, f32[384]{0:T(512)}, f32[768]{0:T(1024)}) custom-call(f32[48,4096]{1,0:T(8,128)S(1)} %get-tuple-element.6.t_in, f32[1,384]{1,0:T(1,128)S(1)} %get-tuple-element.7.f_in, f32[1,768]{1,0:T(1,128)S(1)} %get-tuple-element.8.g_in), custom_call_target="tpu_custom_call" | custom-call | tf_op jit(solution)/shard_map/hand_out/pallas_call | solution.py:691

commit v8 on v7

--- a/solution.py
+++ b/solution.py
@@ -21,7 +21,7 @@
 BLK = 96
 NB = COLS // BLK
 PIECE = OWN // 2
-LO_AT = (0, 256, 496, 672, 768)
+LO_AT = (0, 64, 320, 384, 560, 768)
 NSAMP = 6144
 LOGN = math.log(NSAMP)
 SCALE = 1.0 / (WIDTH * EPS)
@@ -212,10 +212,15 @@
         got_x(xo + at_x(3), k)
         send_x(xo + at_x(3), k, XP)
         got_y(slot(3, "o"), k)
-        send_y(slot(3, "o"), k, ZP)
+        if k == 0:
+            send_y(slot(3, "o"), 0, ZP)
         got_y(slot(0, "b"), k)
-        send_y(slot(0, "b"), k, ZM)
+        if k == 0:
+            send_y(slot(0, "b"), 0, ZM)
+            send_y(slot(0, "b"), 0, ZP)
         got_y(slot(1, "o"), k)
+        if k == 1:
+            send_y(slot(1, "o"), 1, ZM)
         got_x(xo + at_x(1), k)
     for k in range(2):
         send_x(xa + x, k, XP)
@@ -235,7 +240,8 @@
         send_x(xa + at_x(1), k, XM)
         got_x(xo + at_x(2), k)
         got_y(slot(2, "o"), k)
-        got_y(slot(1, "b"), k)
+    got_y(slot(1, "b"), 0)
+    got_y(slot(3, "b"), 0)
     for k in range(2):
         send_y(slot(2, "o"), k, PB)
 
@@ -277,17 +283,22 @@
 
     for k in range(2):
         got_y(slot(0, "c"), k)
-        send_y(slot(0, "c"), k, ZP)
-        if k:
+        if k == 0:
+            send_y(slot(0, "c"), 0, ZM)
+        else:
             pair_first(1, kc)
+        got_y(slot(3, "a"), k)
+        if k == 0:
+            send_y(slot(3, "a"), 0, ZP)
+            send_y(slot(0, "c"), 0, ZP)
         got_y(slot(1, "a"), k)
-        send_y(slot(1, "a"), k, ZM)
-        got_y(slot(3, "a"), k)
+        if k == 1:
+            send_y(slot(1, "a"), 1, ZM)
         got_x(xa + at_x(3), k)
         got_x(xa + at_x(2), k)
-    for k in range(2):
-        send_y(slot(0, "b"), k, ZP)
-        send_y(slot(0, "c"), k, ZM)
+    for to in (ZP, ZM):
+        send_y(slot(0, "c"), 1, to)
+        send_y(slot(0, "b"), 1, to)
 
     def split_third(i, c):
         split_x(xa + at_x(2 + i))
@@ -314,16 +325,12 @@
         pair_block(1 + 2 * i, 0)
         return c
 
-    def group2(i, c):
-        pair_block(2 + i, i)
-        return c
-
     def group3(i, c):
         own_block(i, 0)
         return c
 
     def group4(i, c):
-        pair_block(1 + i, 1)
+        pair_block(1 + 2 * i, 1)
         return c
 
     def group5(i, c):
@@ -336,16 +343,32 @@
     for k in range(2):
         got_y(slot(2, "a"), k)
         send_y(slot(2, "a"), k, PB)
+    for k in range(2):
+        got_y(slot(2, "b"), k)
+    pair_block(2, 0)
+    lax.fori_loop(0, 4, group3, 0)
+    for k in range(2):
+        got_y(slot(1, "c"), k)
         got_y(slot(3, "c"), k)
-        got_y(slot(2, "b"), k)
-    lax.fori_loop(0, 2, group2, 0)
-    lax.fori_loop(0, 4, group3, 0)
-    for k in range(2):
-        got_y(slot(1, "c"), k)
+    lax.fori_loop(0, 2, group4, 0)
+    for k in range(2):
         got_y(slot(2, "c"), k)
-        got_y(slot(3, "b"), k)
-    lax.fori_loop(0, 2, group4, 0)
+    pair_block(2, 1)
+    got_y(slot(1, "b"), 1)
+    got_y(slot(3, "b"), 1)
     lax.fori_loop(0, 4, group5, 0)
+
+    def rows_from(k, count):
+        half = k // 384
+        return pl.ds(pl.multiple_of(((1 - half) * yhi + half * (1 - yhi)) * 384 + k - half * 384, 16), count)
+
+    def send_logits(k):
+        at = rows_from(LO_AT[k], LO_AT[k + 1] - LO_AT[k])
+        send(lg.at[at], lo.at[at], los.at[k], pa, lsem.at[2])
+
+    def got_logits(k):
+        at = rows_from(LO_AT[k], LO_AT[k + 1] - LO_AT[k])
+        arrived(lo.at[at], los.at[k])
 
     def pair_wait(i, c):
         m8, s8 = c
@@ -359,15 +382,9 @@
         top = jnp.maximum(m8, jnp.max(v, axis=0))
         return top, s8 * jnp.exp(m8 - top) + jnp.sum(jnp.exp(v - top[None]), axis=0)
 
-    m8, s8 = lax.fori_loop(0, NB, pair_wait, (jnp.full((8, ROWS), -1e30, F32), jnp.zeros((8, ROWS), F32)))
-
-    def send_logits(k):
-        at = pl.ds(LO_AT[k], LO_AT[k + 1] - LO_AT[k])
-        send(lg.at[at], lo.at[at], los.at[k], pa, lsem.at[2])
-
-    def got_logits(k):
-        at = pl.ds(LO_AT[k], LO_AT[k + 1] - LO_AT[k])
-        arrived(lo.at[at], los.at[k])
+    stats = lax.fori_loop(0, NB // 2, pair_wait, (jnp.full((8, ROWS), -1e30, F32), jnp.zeros((8, ROWS), F32)))
+    send_logits(0)
+    m8, s8 = lax.fori_loop(NB // 2, NB, pair_wait, stats)
 
     def exchange(buf, sems, rnd, mine, peers, msg):
         buf[rnd, mine] = msg
@@ -409,7 +426,7 @@
     m = jnp.max(m8, axis=0, keepdims=True)
     tot = jnp.sum(s8 * jnp.exp(m8 - m), axis=0, keepdims=True)
     done = ex_rows(0, row_msg(rows3(m) + rows3(tot)))
-    send_logits(0)
+    send_logits(1)
     everyone = done()
     mm = everyone[:, 0:3, :]
     top = jnp.max(mm, axis=0)
@@ -479,27 +496,30 @@
 
     def far(some):
         for q in some:
-            at = slice(128 * q, 128 * q + 128)
-            po[:, at] = jnp.exp(lo[at, :] + f1 + unpack(go[1], 16 * q, 16)).T
+            at = rows_from(128 * q, 128)
+            lane = lax.broadcasted_iota(jnp.int32, (16, 8, 128), 2)
+            lead = lax.broadcasted_iota(jnp.int32, (16, 8, 128), 0) + at.start // 8
+            g = jnp.sum(jnp.where(lane == lead, go[1][None], 0.0), axis=2, keepdims=True).reshape(128, 1)
+            po[:, pl.ds(pl.multiple_of(at.start, 128), 128)] = jnp.exp(lo[at, :] + f1 + g).T
 
     def in_row1():
-        send_logits(1)
+        send_logits(2)
+        send_logits(3)
         turn(q_, pn, range(0, 3))
 
     def in_row2():
-        send_logits(2)
+        send_logits(4)
         arrived(go.at[1], gs.at[0])
         got_logits(0)
+        got_logits(1)
         far(range(0, 2))
 
     def in_col2():
-        send_logits(3)
-        got_logits(1)
-        far(range(2, 3))
         got_logits(2)
-        far(range(3, 5))
         got_logits(3)
-        far(range(5, 6))
+        far(range(2, 4))
+        got_logits(4)
+        far(range(4, 6))
 
     u = row_step(1, s8, in_row1)
     v = col_step(0, u, lambda: turn(q_, pn, range(3, 6)))
@@ -661,7 +681,7 @@
         dma((16, 2)),
         dma((16,)),
         dma((NB,)),
-        dma((4,)),
+        dma((5,)),
         dma((5,)),
         dma((2, 4)),
         dma((2, 1)),

time: 127 us -> 126 us (level)
  no operation moved by 1% of the time
where the time goes in v8:
time: 126 us
  Pallas kernels  125 us (99%)
    pallas_call x1, Pallas kernels, body(): pl.pallas_call(kernel, out_shape=(vm((OWN, WIDTH), F32), vm((1, ROWS), F3...  123 us

profile of v8, /device:TPU:0, one launch (start us, length us, event | category | flops | bytes accessed | tf_op | source)
XLA Modules:
  0.0 125.7 jit_solution(5537362440032362108)
XLA Ops:
  0.6 123.4 %coupling.1 = (f32[48,4096]{1,0:T(8,128)S(1)}, f32[1,384]{1,0:T(1,128)S(1)}, f32[1,768]{1,0:T(1,128)S(1)}) custom-call(f32[48,4096]{1,0:T(8,128)} %x_hbm.1, f32[48,4096]{1,0:T(8,128)} %y_hbm.1), custom_call_target="tpu_custom_call" | custom-call | tf_op jit(solution)/shard_map/coupling/pallas_call | solution.py:696
  124.1 1.5 %hand_out.1 = (f32[48,4096]{1,0:T(8,128)}, f32[384]{0:T(512)}, f32[768]{0:T(1024)}) custom-call(f32[48,4096]{1,0:T(8,128)S(1)} %get-tuple-element.6.t_in, f32[1,384]{1,0:T(1,128)S(1)} %get-tuple-element.7.f_in, f32[1,768]{1,0:T(1,128)S(1)} %get-tuple-element.8.g_in), custom_call_target="tpu_custom_call" | custom-call | tf_op jit(solution)/shard_map/hand_out/pallas_call | solution.py:711

commit v9 on v8

--- a/solution.py
+++ b/solution.py
@@ -334,7 +334,7 @@
         return c
 
     def group5(i, c):
-        own_block(i, 1)
+        own_block(lax.rem(i + 2, 4), (i + 2) // 4)
         return c
 
     pair_rest(0, ka)
@@ -346,7 +346,7 @@
     for k in range(2):
         got_y(slot(2, "b"), k)
     pair_block(2, 0)
-    lax.fori_loop(0, 4, group3, 0)
+    lax.fori_loop(0, 2, group3, 0)
     for k in range(2):
         got_y(slot(1, "c"), k)
         got_y(slot(3, "c"), k)
@@ -356,7 +356,7 @@
     pair_block(2, 1)
     got_y(slot(1, "b"), 1)
     got_y(slot(3, "b"), 1)
-    lax.fori_loop(0, 4, group5, 0)
+    lax.fori_loop(0, 6, group5, 0)
 
     def rows_from(k, count):
         half = k // 384

time: 126 us -> 124 us (0.984)
  Pallas kernels: 125 us -> 123 us
    pallas_call x1, Pallas kernels: 123 us -> 122 us  [body(): pl.pallas_call(kernel, out_shape=(vm((OWN, WIDTH), F32), vm((1, ROWS), F3...]
where the time goes in v9:
time: 124 us
  Pallas kernels  123 us (99%)
    pallas_call x1, Pallas kernels, body(): pl.pallas_call(kernel, out_shape=(vm((OWN, WIDTH), F32), vm((1, ROWS), F3...  122 us

profile of v9, /device:TPU:0, one launch (start us, length us, event | category | flops | bytes accessed | tf_op | source)
XLA Modules:
  0.0 124.0 jit_solution(16228001869689256973)
XLA Ops:
  0.6 121.7 %coupling.1 = (f32[48,4096]{1,0:T(8,128)S(1)}, f32[1,384]{1,0:T(1,128)S(1)}, f32[1,768]{1,0:T(1,128)S(1)}) custom-call(f32[48,4096]{1,0:T(8,128)} %x_hbm.1, f32[48,4096]{1,0:T(8,128)} %y_hbm.1), custom_call_target="tpu_custom_call" | custom-call | tf_op jit(solution)/shard_map/coupling/pallas_call | solution.py:696
  122.3 1.5 %hand_out.1 = (f32[48,4096]{1,0:T(8,128)}, f32[384]{0:T(512)}, f32[768]{0:T(1024)}) custom-call(f32[48,4096]{1,0:T(8,128)S(1)} %get-tuple-element.6.t_in, f32[1,384]{1,0:T(1,128)S(1)} %get-tuple-element.7.f_in, f32[1,768]{1,0:T(1,128)S(1)} %get-tuple-element.8.g_in), custom_call_target="tpu_custom_call" | custom-call | tf_op jit(solution)/shard_map/hand_out/pallas_call | solution.py:711

commit v10 on v9

--- a/solution.py
+++ b/solution.py
@@ -596,12 +596,13 @@
         compute(c)
         start_pair(c)
         start_own(c)
-        if c:
-            pass_pair(c - 1)
+        if c < 2:
+            last_own(c)
         else:
-            last_own(c)
-    pass_pair(CH - 1)
-    for c in range(1, CH):
+            pass_pair(c - 2)
+    for c in range(CH - 2, CH):
+        pass_pair(c)
+    for c in range(2, CH):
         last_own(c)
 
     fin = flat3(jnp.sum(total()[:, 0:3, :], axis=0))

time: 124 us -> 124 us (level)
  no operation moved by 1% of the time
where the time goes in v10:
time: 124 us
  Pallas kernels  123 us (99%)
    pallas_call x1, Pallas kernels, body(): pl.pallas_call(kernel, out_shape=(vm((OWN, WIDTH), F32), vm((1, ROWS), F3...  122 us

profile of v10, /device:TPU:0, one launch (start us, length us, event | category | flops | bytes accessed | tf_op | source)
XLA Modules:
  0.0 123.8 jit_solution(9865287719882554344)
XLA Ops:
  0.6 121.5 %coupling.1 = (f32[48,4096]{1,0:T(8,128)S(1)}, f32[1,384]{1,0:T(1,128)S(1)}, f32[1,768]{1,0:T(1,128)S(1)}) custom-call(f32[48,4096]{1,0:T(8,128)} %x_hbm.1, f32[48,4096]{1,0:T(8,128)} %y_hbm.1), custom_call_target="tpu_custom_call" | custom-call | tf_op jit(solution)/shard_map/coupling/pallas_call | solution.py:697
  122.2 1.5 %hand_out.1 = (f32[48,4096]{1,0:T(8,128)}, f32[384]{0:T(512)}, f32[768]{0:T(1024)}) custom-call(f32[48,4096]{1,0:T(8,128)S(1)} %get-tuple-element.6.t_in, f32[1,384]{1,0:T(1,128)S(1)} %get-tuple-element.7.f_in, f32[1,768]{1,0:T(1,128)S(1)} %get-tuple-element.8.g_in), custom_call_target="tpu_custom_call" | custom-call | tf_op jit(solution)/shard_map/hand_out/pallas_call | solution.py:712

commit v11 on v10

--- a/solution.py
+++ b/solution.py
@@ -407,8 +407,14 @@
         return done
 
     small = []
-    row_peers = [(n, lax.rem(d + k, 8)) for k in range(1, 8)]
-    col_peers = [col_dev(lax.rem(n + k, 16)) for k in range(1, 16)]
+    row_peers = [(n, lax.rem(ylo + f, 2) * 4 + at_x(dx)) for dx in (2, 1, 3, 0) for f in (1, 0) if dx or f]
+    col_peers = [
+        col_dev((lax.rem(yhi + f, 2) * 4 + at_z(dz)) * 2 + lax.rem(core + o, 2))
+        for dz in (2, 1, 3, 0)
+        for f in (1, 0)
+        for o in (1, 0)
+        if dz or f or o
+    ]
 
     def ex_rows(rnd, msg):
         return exchange(rx, rxs, rnd, d, row_peers, msg)

time: 124 us -> 124 us (level)
  no operation moved by 1% of the time
where the time goes in v11:
time: 124 us; the launch traced here: 123 us
  Pallas kernels  123 us (99%)
    pallas_call x1, Pallas kernels, body(): pl.pallas_call(kernel, out_shape=(vm((OWN, WIDTH), F32), vm((1, ROWS), F3...  121 us

profile of v11, /device:TPU:0, one launch (start us, length us, event | category | flops | bytes accessed | tf_op | source)
XLA Modules:
  0.0 123.4 jit_solution(10941220084612665252)
XLA Ops:
  0.6 121.1 %coupling.1 = (f32[48,4096]{1,0:T(8,128)S(1)}, f32[1,384]{1,0:T(1,128)S(1)}, f32[1,768]{1,0:T(1,128)S(1)}) custom-call(f32[48,4096]{1,0:T(8,128)} %x_hbm.1, f32[48,4096]{1,0:T(8,128)} %y_hbm.1), custom_call_target="tpu_custom_call" | custom-call | tf_op jit(solution)/shard_map/coupling/pallas_call | solution.py:703
  121.7 1.5 %hand_out.1 = (f32[48,4096]{1,0:T(8,128)}, f32[384]{0:T(512)}, f32[768]{0:T(1024)}) custom-call(f32[48,4096]{1,0:T(8,128)S(1)} %get-tuple-element.6.t_in, f32[1,384]{1,0:T(1,128)S(1)} %get-tuple-element.7.f_in, f32[1,768]{1,0:T(1,128)S(1)} %get-tuple-element.8.g_in), custom_call_target="tpu_custom_call" | custom-call | tf_op jit(solution)/shard_map/hand_out/pallas_call | solution.py:718
